TPU v7x, 256 devices: a whole 4x4x8 slice. The times are simulated.
256 devices in a mesh: lon: 16 (over x_lo, z), lat: 8 (over y, core), ens: 2 (over x_hi).
Axes of the slice: x: 4 (x_hi: 2, x_lo: 2; x = x_hi * 2 + x_lo), y: 4, z: 8, core: 2. Of those that a mesh axis runs over, the one named last changes fastest.
Arguments:
- temp: float32 [2, 12, 128, 2048], P('ens', None, 'lat', 'lon'), may hold values from -6 to 6
- height: float32 [2, 128, 2048], P('ens', 'lat', 'lon'), may hold values from -6 to 6
- flow: float32 [2, 2, 128, 2048], P('ens', None, 'lat', 'lon'), may hold values from -6 to 6
- land_sea: int32 [128, 2048], P('lat', 'lon'), may hold values 0 or 1
- fold: int32 [2048], replicated, may hold values from 0 to 2047, as said below
- w_first: bfloat16 [16, 99], replicated, may hold values from -0.625 to 0.625
- w_second: bfloat16 [16, 144], replicated, may hold values from -0.5 to 0.5
- w_third: bfloat16 [10, 144], replicated, may hold values from -0.5 to 0.5
- temp_bar: float32 [2, 12, 128, 2048], P('ens', None, 'lat', 'lon'), may hold values from -6 to 6
- height_bar: float32 [2, 128, 2048], P('ens', 'lat', 'lon'), may hold values from -6 to 6
- flow_bar: float32 [2, 2, 128, 2048], P('ens', None, 'lat', 'lon'), may hold values from -6 to 6
Outputs:
- temp_grad: float32 [2, 12, 128, 2048], P('ens', None, 'lat', 'lon')
- height_grad: float32 [2, 128, 2048], P('ens', 'lat', 'lon')
- flow_grad: float32 [2, 2, 128, 2048], P('ens', None, 'lat', 'lon')
- first_grad: float32 [16, 99], replicated
- second_grad: float32 [16, 144], replicated
- third_grad: float32 [10, 144], replicated
Inputs may be any that keep to these rules, and one draw needn't show every extreme that they name: fold[i] = (s - 1 - i) mod 2048 for one s of each draw, so that fold[fold[i]] = i.
All inputs are finite; a program needn't handle non-finite values. No bound on the sum of `land_sea` on one device may be relied on, other than what follows from the above.
Results may differ from a plain program's by a relative error of at most 0.008.
Values sent between devices are 32-bit elements; how exact they have to be, the bound alone decides.
A program may use at most 128 MiB of HBM per device.

v0:
```python
import math

import jax
import jax.numpy as jnp
from jax import lax
from jax.sharding import PartitionSpec as P

SUB = 4
LAYERS = 3


gravity = 0.3
drag_rate = 0.05
coriolis = 0.2
diffusion = 0.1
advection = 0.1
closure_gain = 0.5


def with_halo(x, sides, width):
    for axis, dim in sides:
        size, length = (lax.axis_size(axis), x.shape[dim])
        up = [(i, (i + 1) % size) for i in range(size)]
        down = [(j, i) for i, j in up]
        last = lax.slice_in_dim(x, length - width, length, axis=dim)
        leading = lax.slice_in_dim(x, 0, width, axis=dim)
        before = lax.ppermute(last, axis, up)
        after = lax.ppermute(leading, axis, down)
        x = jnp.concatenate([before, x, after], axis=dim)
    return x


def crop(field, width):
    return field[..., width : field.shape[-2] - width, width : field.shape[-1] - width]


def physics(tracer_ext, height, east, north, wet):
    for index in range(SUB):
        wet = crop(wet, 1)
        spread = 0.5 * (east[1:-1, 2:] - east[1:-1, :-2]) + 0.5 * (
            north[2:, 1:-1] - north[:-2, 1:-1]
        )
        height = wet * (crop(height, 1) - gravity * spread)
        wet = crop(wet, 1)
        east_old = crop(east, 2)
        north_old = crop(north, 2)
        slope_east = 0.5 * (height[1:-1, 2:] - height[1:-1, :-2])
        slope_north = 0.5 * (height[2:, 1:-1] - height[:-2, 1:-1])
        east = wet * ((1.0 - drag_rate) * east_old - gravity * slope_east + coriolis * north_old)
        north = wet * ((1.0 - drag_rate) * north_old - gravity * slope_north - coriolis * east_old)
        height = crop(height, 1)
    near = crop(tracer_ext, LAYERS - 1)
    centre = near[:, 1:-1, 1:-1]
    laplace = (
        near[:, 2:, 1:-1]
        + near[:, :-2, 1:-1]
        + near[:, 1:-1, 2:]
        + near[:, 1:-1, :-2]
        - 4.0 * centre
    )
    slope_east = 0.5 * (near[:, 1:-1, 2:] - near[:, 1:-1, :-2])
    slope_north = 0.5 * (near[:, 2:, 1:-1] - near[:, :-2, 1:-1])
    east_inner = crop(east, LAYERS)
    north_inner = crop(north, LAYERS)
    wet_inner = crop(wet, LAYERS)
    moved = centre + wet_inner * (
        diffusion * laplace - advection * (east_inner * slope_east + north_inner * slope_north)
    )
    return (moved, height, east_inner, north_inner)


def patches(field):
    channels = field.shape[0]
    row_count = field.shape[1] - 2
    column_count = field.shape[2] - 2
    parts = [
        field[:, down : down + row_count, across : across + column_count]
        for down in range(3)
        for across in range(3)
    ]
    return (
        jnp.concatenate(parts, axis=0).reshape(9 * channels, row_count * column_count),
        row_count,
        column_count,
    )


def unpatch(grads, channels, row_count, column_count):
    grads = grads.reshape(9, channels, row_count, column_count)
    total = jnp.zeros((channels, row_count + 2, column_count + 2), jnp.float32)
    for down in range(3):
        for across in range(3):
            total = total + jnp.pad(
                grads[3 * down + across], ((0, 0), (down, 2 - down), (across, 2 - across))
            )
    return total


def contract_last(left, right):
    return lax.dot_general(
        left, right, (((1,), (1,)), ((), ())), preferred_element_type=jnp.float32
    )


def contract_first(left, right):
    return lax.dot_general(
        left, right, (((0,), (0,)), ((), ())), preferred_element_type=jnp.float32
    )


def closure_forward(inputs, weights):
    w_first, w_second, w_third = weights
    first, rows_one, columns_one = patches(inputs)
    act_one = jnp.tanh(jnp.dot(w_first, first, preferred_element_type=jnp.float32))
    hidden_one = act_one.astype(jnp.bfloat16).reshape(act_one.shape[0], rows_one, columns_one)
    second, rows_two, columns_two = patches(hidden_one)
    act_two = jnp.tanh(jnp.dot(w_second, second, preferred_element_type=jnp.float32))
    hidden_two = act_two.astype(jnp.bfloat16).reshape(act_two.shape[0], rows_two, columns_two)
    third, rows_three, columns_three = patches(hidden_two)
    extents = (rows_one, columns_one, rows_two, columns_two, rows_three, columns_three)
    return (first, act_one, second, act_two, third, extents)


def closure_backward(grad_tendency, saved, weights):
    w_first, w_second, w_third = weights
    first, act_one, second, act_two, third, extents = saved
    rows_one, columns_one, rows_two, columns_two, rows_three, columns_three = extents
    grad_three = grad_tendency.astype(jnp.bfloat16)
    weight_three = contract_last(grad_three, third)
    back_three = unpatch(
        contract_first(w_third, grad_three), act_two.shape[0], rows_three, columns_three
    )
    grad_two = (back_three.reshape(act_two.shape) * (1.0 - act_two * act_two)).astype(jnp.bfloat16)
    weight_two = contract_last(grad_two, second)
    back_two = unpatch(contract_first(w_second, grad_two), act_one.shape[0], rows_two, columns_two)
    grad_one = (back_two.reshape(act_one.shape) * (1.0 - act_one * act_one)).astype(jnp.bfloat16)
    weight_one = contract_last(grad_one, first)
    back_one = unpatch(
        contract_first(w_first, grad_one), first.shape[0] // 9, rows_one, columns_one
    )
    return (back_one, (weight_one, weight_two, weight_three))


def local_adjoint(
    tracer_ext, height, east, north, wet, weights, temp_bar, height_bar, east_bar, north_bar
):
    levels = temp_bar.shape[0]
    closed = weights[2].shape[0]

    def advance(tracer_in, height_in, east_in, north_in):
        return physics(tracer_in, height_in, east_in, north_in, wet)

    outputs, pull = jax.vjp(advance, tracer_ext, height, east, north)
    height_rim = outputs[1]
    inputs = jnp.concatenate([tracer_ext[:closed], height_rim[None]], axis=0).astype(jnp.bfloat16)
    saved = closure_forward(inputs, weights)
    wet_inner = crop(wet, (wet.shape[-1] - temp_bar.shape[-1]) // 2)
    grad_tendency = (closure_gain * wet_inner * temp_bar[:closed]).reshape(closed, -1)
    back_inputs, weight_grads = closure_backward(grad_tendency, saved, weights)
    height_rim_grad = back_inputs[closed] + jnp.pad(height_bar, LAYERS)
    tracer_grad, height_ext, east_ext, north_ext = pull(
        (temp_bar, height_rim_grad, east_bar, north_bar)
    )
    tracer_grad = tracer_grad + jnp.pad(
        back_inputs[:closed], ((0, levels - closed), (0, 0), (0, 0))
    )
    return (tracer_grad, height_ext, east_ext, north_ext, weight_grads)


def fill_edges(extended, gathered, width, signs, context):
    fold, lon_pos, lon_count, lat_cells, lon_cells, is_top, is_bottom = context
    lon_total = fold.shape[0]
    span = (
        lon_pos * lon_cells + jnp.arange(-width, lon_cells + width, dtype=jnp.int32)
    ) % lon_total
    source = jnp.take(fold, span)
    north = signs * jnp.flip(jnp.take(gathered, source, axis=2), axis=1)
    upper = jnp.where(is_top, north, extended[:, lat_cells + width :, :])
    lower = extended[:, :width, :]
    lower = jnp.where(is_bottom, jnp.zeros_like(lower), lower)
    return jnp.concatenate([lower, extended[:, width : lat_cells + width, :], upper], axis=1)


def extend_groups(groups, halo_calls, gather_call, context):
    lat_cells = context[3]
    extended = [
        halo_call(stacked, width) for (stacked, width, signs), halo_call in zip(groups, halo_calls)
    ]
    gathered = gather_call(
        tuple((stacked[:, lat_cells - width :, :] for stacked, width, signs in groups))
    )
    results = []
    for (stacked, width, signs), grown, rows_all in zip(groups, extended, gathered):
        results.append(fill_edges(grown, rows_all, width, signs, context))
    return results


def collect_edges(grown, width, lat_cells, lon_cells):

    def columns(band):
        middle = band[..., 2 * width : lon_cells + 2 * width]
        left = jnp.pad(band[..., :width], ((0, 0), (0, 0), (0, lon_cells - width)))
        right = jnp.pad(
            band[..., lon_cells + 3 * width :], ((0, 0), (0, 0), (lon_cells - width, 0))
        )
        return middle + left + right

    middle = columns(grown[:, 2 * width : lat_cells + 2 * width])
    lower = jnp.pad(columns(grown[:, :width]), ((0, 0), (0, lat_cells - width), (0, 0)))
    upper = jnp.pad(
        columns(grown[:, lat_cells + 3 * width :]), ((0, 0), (lat_cells - width, 0), (0, 0))
    )
    return middle + lower + upper


def fold_back(gathered, width, signs, context):
    fold, lon_pos, lon_count, lat_cells, lon_cells, is_top, is_bottom = context
    lon_total = fold.shape[0]
    span = (
        jnp.arange(lon_count, dtype=jnp.int32)[:, None] * lon_cells
        + jnp.arange(-width, lon_cells + width, dtype=jnp.int32)[None, :]
    ) % lon_total
    column_sums = jax.ops.segment_sum(
        jnp.moveaxis(gathered, 2, 0), span.reshape(-1), num_segments=lon_total
    )
    mine = jnp.take(fold, lon_pos * lon_cells + jnp.arange(lon_cells, dtype=jnp.int32))
    picked = jnp.moveaxis(jnp.take(column_sums, mine, axis=0), 0, 2)
    return signs * jnp.flip(picked, axis=1)


def reduce_groups(groups, halo_calls, gather_call, context):
    fold, lon_pos, lon_count, lat_cells, lon_cells, is_top, is_bottom = context
    totals = []
    norths = []
    for (grads, width, signs), halo_call in zip(groups, halo_calls):
        north = grads[:, lat_cells + width :, :]
        south = grads[:, :width, :]
        outgoing = jnp.concatenate(
            [
                jnp.where(is_bottom, jnp.zeros_like(south), south),
                grads[:, width : lat_cells + width, :],
                jnp.where(is_top, jnp.zeros_like(north), north),
            ],
            axis=1,
        )
        totals.append(collect_edges(halo_call(outgoing, width), width, lat_cells, lon_cells))
        norths.append(north)
    gathered = gather_call(tuple(norths))
    results = []
    for (grads, width, signs), total, rows_all in zip(groups, totals, gathered):
        folded = fold_back(rows_all, width, signs, context)
        upper = jnp.pad(folded, ((0, 0), (lat_cells - width, 0), (0, 0)))
        results.append(total + jnp.where(is_top, upper, jnp.zeros_like(upper)))
    return results


def local(
    temp, height, flow, land_sea, fold, w_first, w_second, w_third, temp_bar, height_bar, flow_bar
):
    levels = temp.shape[1]
    lat_cells = temp.shape[2]
    lon_cells = temp.shape[3]
    rim = 2 * SUB + LAYERS
    lat_count = lax.axis_size("lat")
    lat_pos = lax.axis_index("lat")
    is_top = lat_pos == lat_count - 1
    is_bottom = lat_pos == 0
    lon_count = lax.axis_size("lon")
    lon_pos = lax.axis_index("lon")
    context = (fold, lon_pos, lon_count, lat_cells, lon_cells, is_top, is_bottom)
    surface = jnp.stack([height[0], flow[0, 0], flow[0, 1], land_sea.astype(jnp.float32)])
    surface_signs = jnp.array([1.0, -1.0, -1.0, 1.0], jnp.float32).reshape(4, 1, 1)
    tracer_signs = jnp.ones((levels, 1, 1), jnp.float32)
    joined = jnp.concatenate([temp[0], surface], axis=0)
    joined_signs = jnp.concatenate([tracer_signs, surface_signs], axis=0)
    (joined_ext,) = extend_groups(
        ((joined, rim, joined_signs),),
        (lambda stacked, breadth: with_halo(stacked, (("lon", 2), ("lat", 1)), breadth),),
        lambda parts: (lax.all_gather(parts[0], "lon", axis=2, tiled=True),),
        context,
    )
    tracer_ext = crop(joined_ext[:levels], rim - LAYERS)
    surface_ext = joined_ext[levels:]
    weights = (w_first, w_second, w_third)
    tracer_grad, height_back, east_back, north_back, weight_grads = local_adjoint(
        tracer_ext,
        surface_ext[0],
        surface_ext[1],
        surface_ext[2],
        surface_ext[3],
        weights,
        temp_bar[0],
        height_bar[0],
        flow_bar[0, 0],
        flow_bar[0, 1],
    )
    surface_grad = jnp.stack([height_back, east_back, north_back])
    scale = 1.0 / math.sqrt(lax.axis_size("ens") * lat_count * lat_cells * lon_count * lon_cells)
    summed = lax.psum((weight_grads[0], weight_grads[1], weight_grads[2]), ("lon", "lat", "ens"))
    margin = rim - LAYERS
    joined_grad = jnp.concatenate(
        [jnp.pad(tracer_grad, ((0, 0), (margin, margin), (margin, margin))), surface_grad], axis=0
    )
    joined_signs = jnp.concatenate([tracer_signs, surface_signs[:3]], axis=0)
    (joined_out,) = reduce_groups(
        ((joined_grad, rim, joined_signs),),
        (lambda stacked, breadth: with_halo(stacked, (("lon", 2), ("lat", 1)), breadth),),
        lambda parts: (lax.all_gather(parts[0], "lon", axis=2, tiled=True),),
        context,
    )
    tracer_out = joined_out[:levels]
    surface_out = joined_out[levels:]
    return (
        tracer_out[None],
        surface_out[0][None],
        surface_out[1:3][None],
        summed[0] * scale,
        summed[1] * scale,
        summed[2] * scale,
    )


def solution(mesh):
    in_specs = (
        P("ens", None, "lat", "lon"),
        P("ens", "lat", "lon"),
        P("ens", None, "lat", "lon"),
        P("lat", "lon"),
        P(),
        P(),
        P(),
        P(),
        P("ens", None, "lat", "lon"),
        P("ens", "lat", "lon"),
        P("ens", None, "lat", "lon"),
    )
    out_specs = (
        P("ens", None, "lat", "lon"),
        P("ens", "lat", "lon"),
        P("ens", None, "lat", "lon"),
        P(),
        P(),
        P(),
    )
    return jax.shard_map(local, mesh=mesh, in_specs=in_specs, out_specs=out_specs, check_vma=False)
```

profile of v0, /device:TPU:1, one launch (start us, length us, event | category | flops | bytes accessed | tf_op | source)
XLA Modules:
  0.0 793.5 jit_solution(4541118509919456048)
XLA Ops:
  11.8 2.5 collective-permute-start
  14.4 5.0 collective-permute-start.1
  19.4 1.6 gather_fusion.2
  21.0 1.4 gather_fusion
  25.9 2.1 collective-permute-start.2
  28.7 1.7 collective-permute-done.2
  30.6 42.2 %all-gather.3.cloned.1.call-done = f32[16,11,2048]{2,0,1:T(8,128)} async-done(((f32[16,11,128]{2,0,1:T(8,128)}), f32[16,11,2048]{2,0,1:T(8,128)}) %all-gather.3.cloned.1.call-update) | async-done | bytes 1441808 | tf_op jit(solution)/shard_map/all_gather | solution.py:279
  72.8 12.4 %copy.657 = f32[16,11,2048]{1,0,2:T(8,128)} copy(f32[16,11,2048]{2,0,1:T(8,128)} %all-gather.3.cloned.1.call-done) | data formatting | bytes 2883584 | tf_op jit(solution)/shard_map/all_gather | solution.py:279
  85.2 6.5 gather_fusion.1
  102.7 1.3 pad_maximum_fusion.8
  105.4 1.4 copy.681
  106.7 2.2 copy.682
  108.9 2.1 copy.683
  111.0 2.1 copy.684
  113.2 2.2 copy.685
  115.3 2.1 copy.686
  117.5 7.4 concatenate.54
  124.9 1.4 reshape.324
  134.0 2.8 reshape.370
  138.1 0.9 fusion.115
  139.2 1.1 squeeze.134
  140.3 1.9 squeeze.133
  142.2 1.9 squeeze.132
  144.0 1.9 squeeze.131
  145.9 1.9 squeeze.130
  147.8 1.9 squeeze.129
  149.7 0.9 squeeze.128
  151.5 2.4 pad_add_fusion
  156.0 1.1 squeeze.141
  157.1 1.8 squeeze.140
  158.9 1.8 squeeze.139
  160.7 1.8 squeeze.138
  162.5 1.8 squeeze.137
  165.2 1.8 pad_add_fusion.4
  167.2 1.2 fusion.88
  168.6 1.8 fusion.26
  179.5 1.8 copy.704
  182.1 1.2 collective-permute-start.4
  183.3 2.5 collective-permute-start.5
  187.8 1.3 fusion.2
  189.7 280.3 %all-reduce.99 = (f32[16,99]{1,0:T(8,128)S(1)}, f32[16,144]{1,0:T(8,128)S(1)}, f32[10,144]{1,0:T(8,128)S(1)}) all-reduce(f32[16,99]{1,0:T(8,128)S(1)} %fusion.124, f32[16,144]{1,0:T(8,128)S(1)} %fusion.125, f32[10,144]{1,0:T(8,128)S(1)} %fusion.2), channel_id=1, replica_groups=mesh['lon'=16,'lat'=8,'ens'=2] {'lon','lat','ens'}, use_global_device_ids=true, to_apply=%region_3.4 | all-reduce | flops 5328 | bytes 42624 | tf_op jit(solution)/shard_map/psum | solution.py:299
  471.2 1.2 pad_maximum_fusion.7
  473.3 1.1 collective-permute-start.6
  475.0 0.9 slice.834
  476.0 1.6 collective-permute-done.7
  478.2 6.1 broadcast_in_dim.69
  484.3 293.1 %scatter_fusion = f32[2048,15,11]{2,1,0:T(8,128)} fusion(f32[2048,15,11]{2,1,0:T(8,128)} %broadcast_in_dim.69, s32[2400]{0:T(1024)S(1)} %fusion.91, f32[2400,15,11]{2,1,0:T(8,128)} %bitcast.158), kind=kCustom, calls=%fused_computation.4 | custom fusion | flops 396000 | bytes 4761600 | tf_op jit(solution)/shard_map/scatter-add | solution.py:223
  777.4 6.6 gather_fusion.3
  (286 shorter events, 52.1 us)
Async XLA Ops:
  7.2 129.6 %copy-start = (bf16[16,144]{1,0:T(8,128)(2,1)S(1)}, bf16[16,144]{1,0:T(8,128)(2,1)}, u32[]{:S(2)}) copy-start(bf16[16,144]{1,0:T(8,128)(2,1)} %param.18) | copy-start | bytes 13828
  7.2 13.8 %copy-start.2 = (s32[2048]{0:T(1024)S(1)}, s32[2048]{0:T(1024)}, u32[]{:S(2)}) copy-start(s32[2048]{0:T(1024)} %param.16) | copy-start | bytes 24580
  7.2 16.1 %copy-start.30 = (f32[1,2,16,128]{3,2,1,0:T(8,128)S(1)}, f32[1,2,16,128]{3,2,1,0:T(8,128)}, u32[]{:S(2)}) copy-start(f32[1,2,16,128]{3,2,1,0:T(8,128)} %param.22) | copy-start | bytes 49156
  7.2 17.6 %copy-start.33 = (f32[1,16,128]{2,1,0:T(8,128)S(1)}, f32[1,16,128]{2,1,0:T(8,128)}, u32[]{:S(2)}) copy-start(f32[1,16,128]{2,1,0:T(8,128)} %param.21) | copy-start | bytes 24580
  7.2 65.6 %all-gather.3.cloned.1.call-start = ((), (), s32[]{:S(2)}) async-start(), calls=%async_computation | async-start | bytes 1531904 | tf_op jit(solution)/shard_map/all_gather | solution.py:279
  11.7 466.6 %all-gather.5.cloned.1.call-start = ((), (), s32[]{:S(2)}) async-start(), calls=%async_computation.1 | async-start | bytes 20889600 | tf_op jit(solution)/shard_map/all_gather | solution.py:308
  11.8 13.7 %collective-permute-start = (f32[16,16,11]{2,1,0:T(8,128)S(1)}, f32[16,16,11]{2,1,0:T(8,128)S(1)}, u32[]{:S(2)}, u32[]{:S(2)}) collective-permute-start(f32[16,16,11]{2,1,0:T(8,128)S(1)} %get-tuple-element.166), channel_id=1, source_target_pairs={{0,16},{16,32},{32,48},{48,64},{64,80},{80,96},{96,112},{112,128},... | collective-permute-start | bytes 33800 | tf_op jit(solution)/shard_map/ppermute | solution.py:27
  14.4 11.2 %collective-permute-start.1 = (f32[16,16,11]{2,1,0:T(8,128)S(1)}, f32[16,16,11]{2,1,0:T(8,128)S(1)}, u32[]{:S(2)}, u32[]{:S(2)}) collective-permute-start(f32[16,16,11]{2,1,0:T(8,128)S(1)} %get-tuple-element.167), channel_id=1, source_target_pairs={{16,0},{32,16},{48,32},{64,48},{80,64},{96,80},{112,96},{128,112},... | collective-permute-start | bytes 33800 | tf_op jit(solution)/shard_map/ppermute | solution.py:28
  25.5 67.2 %copy-start.3 = (f32[16,16,11]{2,1,0:T(8,128)}, f32[16,16,11]{2,1,0:T(8,128)S(1)}, u32[]{:S(2)}) copy-start(f32[16,16,11]{2,1,0:T(8,128)S(1)} %collective-permute-done) | copy-start | bytes 33796
  25.5 67.2 %copy-start.5 = (f32[16,16,11]{2,1,0:T(8,128)}, f32[16,16,11]{2,1,0:T(8,128)S(1)}, u32[]{:S(2)}) copy-start(f32[16,16,11]{2,1,0:T(8,128)S(1)} %collective-permute-done.1) | copy-start | bytes 33796
  25.9 4.6 collective-permute-start.2
  28.7 63.8 %collective-permute-start.3 = (f32[16,11,150]{2,0,1:T(8,128)S(1)}, f32[16,11,150]{2,0,1:T(8,128)S(1)}, u32[]{:S(2)}, u32[]{:S(2)}) collective-permute-start(f32[16,11,150]{2,0,1:T(8,128)S(1)} %copy.711), channel_id=1, source_target_pairs={{2,0},{4,2},{6,4},{8,6},{10,8},{12,10},{14,12},{0,14},{3,1},{5,3},... | collective-permute-start | bytes 316808 | tf_op jit(solution)/shard_map/ppermute | solution.py:28
  85.2 7.4 copy-start.38
  95.0 2.0 copy-start.20
  95.1 1.7 copy-start.16
  95.2 1.6 copy-start.14
  95.3 1.7 copy-start.18
  95.7 1.4 copy-start.12
  95.8 1.5 copy-start.10
  96.1 2.6 copy-start.22
  96.6 3.1 copy-start.26
  96.9 3.6 copy-start.34
  117.5 8.8 %copy-start.31 = (bf16[16,99]{1,0:T(8,128)(2,1)S(1)}, bf16[16,99]{1,0:T(8,128)(2,1)}, u32[]{:S(2)}) copy-start(bf16[16,99]{1,0:T(8,128)(2,1)} %param.17) | copy-start | bytes 9508
  131.6 5.2 copy-start.24
  137.7 1.3 copy-start.8
  151.5 2.7 copy-start.32
  164.3 2.8 copy-start.29
  165.2 3.4 copy-start.4
  165.2 3.4 copy-start.6
  168.5 5.0 copy-start.23
  168.6 5.1 copy-start.21
  170.4 3.5 copy-start.19
  172.4 1.7 copy-start.17
  173.5 0.9 copy-start.15
  173.7 0.9 copy-start.13
  173.9 0.9 copy-start.11
  174.4 1.2 copy-start.25
  176.1 0.9 copy-start.27
  178.6 3.5 copy-start.28
  181.3 8.1 %copy-start.9 = (bf16[16,2340]{1,0:T(8,128)(2,1)S(1)}, bf16[16,2340]{1,0:T(8,128)(2,1)}, u32[]{:S(2)}) copy-start(bf16[16,2340]{1,0:T(8,128)(2,1)} %copy-done.8) | copy-start | bytes 224644
  182.1 289.1 %collective-permute-start.4 = (f32[15,38,11]{2,1,0:T(8,128)}, f32[15,38,11]{2,1,0:T(8,128)S(1)}, u32[]{:S(2)}, u32[]{:S(2)}) collective-permute-start(f32[15,38,11]{2,1,0:T(8,128)} %get-tuple-element.140), channel_id=1, source_target_pairs={{0,16},{16,32},{32,48},{48,64},{64,80},{80,96},{96,112},{112,128},... | collective-permute-start | bytes 75248 | tf_op jit(solution)/shard_map/ppermute | solution.py:27
  183.3 287.9 %collective-permute-start.5 = (f32[15,38,11]{2,1,0:T(8,128)}, f32[15,38,11]{2,1,0:T(8,128)}, u32[]{:S(2)}, u32[]{:S(2)}) collective-permute-start(f32[15,38,11]{2,1,0:T(8,128)} %get-tuple-element.141), channel_id=1, source_target_pairs={{16,0},{32,16},{48,32},{64,48},{80,64},{96,80},{112,96},{128,112},... | collective-permute-start | bytes 75248 | tf_op jit(solution)/shard_map/ppermute | solution.py:28
  471.2 6.7 copy-start.36
  472.7 4.9 collective-permute-start.7
  473.3 4.4 collective-permute-start.6
  777.4 7.0 copy-start.37
  777.4 7.1 copy-start.35
  777.4 9.2 %copy-start.1 = (bf16[16,144]{1,0:T(8,128)(2,1)S(1)}, bf16[16,144]{1,0:T(8,128)(2,1)}, u32[]{:S(2)}) copy-start(bf16[16,144]{1,0:T(8,128)(2,1)} %param.18) | copy-start | bytes 13828
  (1 other events, 0.8 us)
Sparse Core Ops, SparseCore 0:
  11.8 60.9 all-gather.2
  181.4 224.5 all-gather.4
where the time goes:
time: 799 us; the launch traced here: 793 us
  other arithmetic  315 us (39%)
  blocking collectives  280 us (35%)
  local copies, waits for them, and re-layouts  118 us (15%)
  waiting for transfers between devices  45.6 us (6%)
  between operations  15.3 us (2%)
  starting transfers between devices  15.2 us (2%)
    scatter-add x1, other arithmetic, fold_back(): jax.ops.segment_sum(jnp.moveaxis(gathered, 2, 0), span.reshape(-1), num_s...  293 us
    psum x1, blocking collectives, local(): lax.psum((weight_grads[0], weight_grads[1], weight_grads[2]), ('lon', 'la...  280 us
    all_gather x2, waiting for transfers between devices, local(): lax.all_gather(parts[0], 'lon', axis=2, tiled=True)  42.3 us
    squeeze x18, local copies, waits for them, and re-layouts, unpatch(): grads[3 * down + across]  22.2 us
    unnamed x138, local copies, waits for them, and re-layouts  18.7 us
  transfers between devices with their start and end apart: 10, of which 3 were waited for; matrix products, arithmetic and copies ran while one was open for 5% of the time, Pallas kernels for 0%

commit v1 on v0

v1 whole, which is shorter than its diff:
```python
import functools
import math

import jax
import jax.numpy as jnp
from jax import lax
from jax.experimental import pallas as pl
from jax.experimental.pallas import tpu as pltpu
from jax.sharding import PartitionSpec as P

MESH = pl.DeviceIdType.MESH
F32 = jnp.float32
BF16 = jnp.bfloat16

SUB = 4
LEV = 12
CL = 10
RIM = 11
TRIM = 3
HCH = 12
LANES = 128

gravity = 0.3
drag_rate = 0.05
coriolis = 0.2
diffusion = 0.1
advection = 0.1
closure_gain = 0.5


def lane_iota(rows):
    return lax.broadcasted_iota(jnp.int32, (rows, LANES), 1)


def east_of(x):
    a, b = (pltpu.roll(v, LANES - 1, 1) for v in x)
    edge = lane_iota(a.shape[0]) == LANES - 1
    return (jnp.where(edge, b, a), jnp.where(edge, a, b))


def west_of(x):
    a, b = (pltpu.roll(v, 1, 1) for v in x)
    edge = lane_iota(a.shape[0]) == 0
    return (jnp.where(edge, b, a), jnp.where(edge, a, b))


def north_of(x):
    return tuple(pltpu.roll(v, v.shape[0] - 1, 0) for v in x)


def south_of(x):
    return tuple(pltpu.roll(v, 1, 0) for v in x)


def lift(fn):
    return lambda *pairs: tuple(fn(*vs) for vs in zip(*pairs))


sub2 = lift(lambda u, v: u - v)


def step_forward(h, e, n, w):
    de = sub2(east_of(e), west_of(e))
    dn = sub2(north_of(n), south_of(n))
    h = lift(lambda w_, h_, a, b: w_ * (h_ - (0.5 * gravity) * (a + b)))(w, h, de, dn)
    se = sub2(east_of(h), west_of(h))
    sn = sub2(north_of(h), south_of(h))
    keep = 1.0 - drag_rate
    e_new = lift(lambda w_, e_, n_, s: w_ * (keep * e_ - (0.5 * gravity) * s + coriolis * n_))(w, e, n, se)
    n_new = lift(lambda w_, e_, n_, s: w_ * (keep * n_ - (0.5 * gravity) * s - coriolis * e_))(w, e, n, sn)
    return h, e_new, n_new


def step_adjoint(h, e, n, w):
    we = lift(lambda a, b: a * b)(w, e)
    wn = lift(lambda a, b: a * b)(w, n)
    de = sub2(east_of(we), west_of(we))
    dn = sub2(north_of(wn), south_of(wn))
    hw = lift(lambda w_, h_, a, b: w_ * (h_ + (0.5 * gravity) * (a + b)))(w, h, de, dn)
    se = sub2(east_of(hw), west_of(hw))
    sn = sub2(north_of(hw), south_of(hw))
    keep = 1.0 - drag_rate
    e_new = lift(lambda a, b, s: keep * a - coriolis * b + (0.5 * gravity) * s)(we, wn, se)
    n_new = lift(lambda a, b, s: keep * b + coriolis * a + (0.5 * gravity) * s)(we, wn, sn)
    return hw, e_new, n_new


def slot_mask(rows, width, count, offset):
    lane = lane_iota(rows)
    mask = None
    for slot in range(count):
        start = 2 * width * slot + offset
        here = (lane >= start) & (lane < start + width)
        mask = here if mask is None else mask | here
    return mask


def pack_edges(fields, width):
    lane = lane_iota(fields[0].shape[0])
    out = jnp.zeros_like(fields[0])
    for slot, field in enumerate(fields):
        start = 2 * width * slot
        rolled = pltpu.roll(field, (start + width) % LANES, 1)
        out = jnp.where((lane >= start) & (lane < start + 2 * width), rolled, out)
    return out


def unpack_edge(packed, width, slot):
    lane = lane_iota(packed.shape[0])
    rolled = pltpu.roll(packed, (-width - 2 * width * slot) % LANES, 1)
    return jnp.where((lane < width) | (lane >= LANES - width), rolled, 0.0)


def split_bf16(x):
    high = x.astype(BF16)
    rest = x - high.astype(F32)
    middle = rest.astype(BF16)
    low = (rest - middle.astype(F32)).astype(BF16)
    return jnp.concatenate([high, middle, low], axis=0)


def permute_columns(x, select):
    rows = x.shape[0]
    y = jnp.dot(split_bf16(x), select, preferred_element_type=F32)
    return (y[2 * rows :] + y[rows : 2 * rows]) + y[:rows]


def store_shifted(ref, row, pair):
    for dx, shifted in enumerate((west_of(pair), pair, east_of(pair))):
        for tile in range(2):
            ref[tile, row, 16 * dx : 16 * dx + 16, :] = shifted[tile].astype(BF16)


def patch(ref, row):
    return jnp.concatenate([ref[tile, row : row + 3].reshape(144, LANES) for tile in range(2)], axis=1)


def conv_row(weight, ref, row):
    y = jnp.dot(weight, patch(ref, row), preferred_element_type=F32)
    return (y[:, :LANES], y[:, LANES:])


def contract(left, right):
    return lax.dot_general(left, right, (((1,), (1,)), ((), ())), preferred_element_type=F32)


def kernel(
    sizes,
    temp,
    height,
    flow,
    land_sea,
    fold,
    w_first,
    w_second,
    w_third,
    temp_bar,
    height_bar,
    flow_bar,
    temp_out,
    height_out,
    flow_out,
    first_out,
    second_out,
    third_out,
    surf,
    trac,
    inputs,
    wet_i,
    bar_t,
    bar_h,
    bar_f,
    fold_s,
    w1_raw,
    w2_raw,
    w3_raw,
    w_rows,
    w_flip,
    msg_out,
    msg_in,
    fold_surf,
    fold_trac,
    g3_rows,
    xs1,
    xs2,
    xs3,
    gs1,
    gs2,
    gs3,
    act1,
    act2,
    back,
    sg,
    tg,
    back_out,
    back_in,
    back_surf,
    back_trac,
    unfold_surf,
    unfold_trac,
    wsum,
    rs_in,
    part_in,
    full,
    load_sem,
    f_send,
    f_recv,
    m_send,
    m_recv,
    fold_send,
    fold_recv,
    b_send,
    b_recv,
    bm_send,
    bm_recv,
    unfold_send,
    unfold_recv,
    ar_send,
    ar_recv,
):
    nlon, nlat, nens = sizes
    lon, lat, ens = lax.axis_index("lon"), lax.axis_index("lat"), lax.axis_index("ens")
    top = nlat - 1
    left, right = lax.rem(lon + nlon - 1, nlon), lax.rem(lon + 1, nlon)
    group = nlat * nens
    place = ens * nlat + lat
    chunk = 64 // nlon

    def remote(src, dst, send, recv, **device):
        return pltpu.make_async_remote_copy(
            src_ref=src, dst_ref=dst, send_sem=send, recv_sem=recv, device_id=device, device_id_type=MESH
        )

    barrier = pltpu.get_barrier_semaphore()

    def greet(**device):
        pl.semaphore_signal(barrier, inc=1, device_id=device, device_id_type=MESH)

    for k in range(1, nlon):
        greet(lon=lax.rem(lon + k, nlon))
    for k in range(1, group):
        other = lax.rem(place + k, group)
        greet(lat=lax.rem(other, nlat), ens=other // nlat)

    @pl.when(lat > 0)
    def _():
        greet(lon=left, lat=lat - 1)
        greet(lon=right, lat=lat - 1)

    @pl.when(lat < top)
    def _():
        greet(lon=left, lat=lat + 1)
        greet(lon=right, lat=lat + 1)

    loads = [
        (temp.at[0], trac.at[0, :, 8:24, :]),
        (height.at[0], surf.at[0, 0, 16:32, :]),
        (flow.at[0], surf.at[0, 1:3, 16:32, :]),
        (land_sea, wet_i),
        (fold, fold_s),
        (w_first, w1_raw),
        (w_second, w2_raw),
        (w_third, w3_raw),
        (temp_bar.at[0], bar_t),
        (height_bar.at[0], bar_h),
        (flow_bar.at[0], bar_f),
    ]
    loads = [pltpu.make_async_copy(src, dst, load_sem.at[k]) for k, (src, dst) in enumerate(loads)]
    for load in loads:
        load.start()

    inputs[:, 32 * (HCH + 1) :, :] = jnp.zeros((2, 32 * (15 - HCH), LANES), F32)
    for ref, rows in ((gs3, 20), (gs2, 22), (gs1, 24)):
        for tile in range(2):
            for row in (0, 1, rows - 2, rows - 1):
                ref[tile, row] = jnp.zeros((48, LANES), BF16)
    back[...] = jnp.zeros_like(back)
    fold_surf[lon, 40:48, :] = jnp.zeros((8, LANES), F32)
    fold_trac[lon, 32:40, :] = jnp.zeros((8, LANES), F32)
    unfold_surf[lon, 32:40, :] = jnp.zeros((8, LANES), F32)
    unfold_trac[lon, 32:40, :] = jnp.zeros((8, LANES), F32)

    @pl.when(lat == 0)
    def _():
        surf[:, :, 0:16, :] = jnp.zeros((2, 4, 16, LANES), F32)
        trac[:, :, 0:8, :] = jnp.zeros((2, LEV, 8, LANES), F32)
        back_in[:, 0] = jnp.zeros((2, 2, 16, LANES), F32)
        back_surf[0] = jnp.zeros((3, 16, LANES), F32)
        back_trac[0] = jnp.zeros((LEV, 8, LANES), F32)

    @pl.when(lat == top)
    def _():
        surf[:, :, 32:48, :] = jnp.zeros((2, 4, 16, LANES), F32)
        trac[:, :, 24:32, :] = jnp.zeros((2, LEV, 8, LANES), F32)
        back_in[:, 2] = jnp.zeros((2, 2, 16, LANES), F32)
        back_surf[1] = jnp.zeros((3, 16, LANES), F32)
        back_trac[1] = jnp.zeros((LEV, 8, LANES), F32)

    for k in (1, 2, 3, 0):
        loads[k].wait()
    surf[0, 3, 16:32, :] = wet_i[...].astype(F32)
    msg_out[0] = pack_edges([surf[0, f, 16:32, :] for f in range(4)], RIM)
    msg_out[1] = pack_edges([trac[0, c, 8:24, :] for c in range(LEV)], TRIM)

    def lat_copies(up):
        to = 1 if up else -1
        rows_s = slice(0, 16) if up else slice(32, 48)
        rows_t = (slice(16, 24), slice(0, 8)) if up else (slice(8, 16), slice(24, 32))
        slot = 0 if up else 2
        return (
            remote(surf.at[0, :, 16:32, :], surf.at[0, :, rows_s, :], f_send.at[slot], f_recv.at[slot], lat=lat + to),
            remote(
                trac.at[0, :, rows_t[0], :],
                trac.at[0, :, rows_t[1], :],
                f_send.at[slot + 1],
                f_recv.at[slot + 1],
                lat=lat + to,
            ),
        )

    def edge_copy(side, shift):
        slot = 3 * side + 1 - shift
        return remote(
            msg_out, msg_in.at[side, 1 - shift], m_send.at[slot], m_recv.at[slot], lon=(right, left)[side], lat=lat + shift
        )

    def fold_copies(k):
        peer = lax.rem(lon + k, nlon)
        return (
            remote(fold_surf.at[lon], fold_surf.at[lon], fold_send.at[0, k], fold_recv.at[0, k], lon=peer),
            remote(fold_trac.at[lon], fold_trac.at[lon], fold_send.at[1, k], fold_recv.at[1, k], lon=peer),
        )

    def fold_arrivals(k):
        source = lax.rem(lon + nlon - k, nlon)
        return (
            remote(fold_surf.at[lon], fold_surf.at[source], fold_send.at[0, k], fold_recv.at[0, k], lon=source),
            remote(fold_trac.at[lon], fold_trac.at[source], fold_send.at[1, k], fold_recv.at[1, k], lon=source),
        )

    @pl.when(lat == top)
    def _():
        for f in range(4):
            for m in range(RIM):
                row = RIM * f + m
                fold_surf[lon, row : row + 1, :] = surf[0, f, 31 - m : 32 - m, :]
        for c in range(LEV):
            for m in range(TRIM):
                row = TRIM * c + m
                fold_trac[lon, row : row + 1, :] = trac[0, c, 23 - m : 24 - m, :]

    pl.semaphore_wait(
        barrier, (nlon - 1) + (group - 1) + 2 * (lat > 0).astype(jnp.int32) + 2 * (lat < top).astype(jnp.int32)
    )

    def for_lat(fn):
        pl.when(lat > 0)(functools.partial(fn, -1))
        fn(0)
        pl.when(lat < top)(functools.partial(fn, 1))

    @pl.when(lat == top)
    def _():
        for k in range(1, nlon):
            fold_copies(k)[0].start()

    def start_forward(shift):
        if shift:
            for copy in lat_copies(shift > 0):
                copy.start()
        for side in range(2):
            edge_copy(side, shift).start()

    for_lat(start_forward)

    @pl.when(lat == top)
    def _():
        for k in range(1, nlon):
            fold_copies(k)[1].start()

    for k in range(4, 11):
        loads[k].wait()
    raw1 = w1_raw[...].astype(F32)
    w_rows[...] = jnp.zeros_like(w_rows)
    for tap in range(9):
        w_rows[0, :, 16 * tap : 16 * tap + CL] = raw1[:, 11 * tap : 11 * tap + CL]
        w_rows[0, :, 16 * tap + HCH : 16 * tap + HCH + 1] = raw1[:, 11 * tap + CL : 11 * tap + CL + 1]
    w_rows[1, :, 0:144] = w2_raw[...].astype(F32)
    w_rows[2, 0:CL, 0:144] = w3_raw[...].astype(F32)
    for layer in range(3):
        first = jnp.transpose(w_rows[layer, :, 0:128])
        second = jnp.transpose(w_rows[layer, :, 128:256])
        for tap in range(9):
            block = second[0:16, :] if tap == 8 else first[16 * tap : 16 * tap + 16, :]
            w_flip[layer, :, 16 * (8 - tap) : 16 * (8 - tap) + 16] = block
    weight1 = w_rows[0, :, 0:144].astype(BF16)
    weight2 = w_rows[1, :, 0:144].astype(BF16)
    flip1, flip2, flip3 = (w_flip[layer].astype(BF16) for layer in range(3))

    wet_own = surf[0, 3, 16:32, :]
    g3_rows[16 * CL :, :] = jnp.zeros((16 * (16 - CL), LANES), F32)
    for c in range(CL):
        g3_rows[16 * c : 16 * c + 16, :] = closure_gain * wet_own * bar_t[c]
    for row in range(16):
        own = g3_rows[pl.ds(row, 16, stride=16), :]
        store_shifted(gs3, row + 2, (own, jnp.zeros_like(own)))

    shift_s = fold_s[0] + 1
    base = shift_s - 139 - LANES * lon + LANES * (2 * nlon)
    tile0 = base // LANES
    offset = shift_s - 1 - LANES * lon + LANES * (2 * nlon) - LANES * tile0

    def mirrored(ref):
        return jnp.concatenate([ref[lax.rem(tile0 + j, nlon)] for j in range(3)], axis=1)

    def mirror_matrix():
        source = lax.broadcasted_iota(jnp.int32, (3 * LANES, 2 * LANES), 0)
        column = lax.broadcasted_iota(jnp.int32, (3 * LANES, 2 * LANES), 1)
        column = jnp.where(column < LANES + LANES // 2, column, column - 2 * LANES)
        return jnp.where(source + column == offset, 1.0, 0.0).astype(BF16)

    left_s = slot_mask(16, RIM, 4, 0)
    left_t = slot_mask(16, TRIM, LEV, 0)

    def wait_forward(shift):
        k = shift + 1
        if shift:
            for copy in lat_copies(shift < 0):
                copy.wait_recv()
        for side in range(2):
            edge_copy(side, -shift).wait_recv()
        packed = jnp.where(left_s, msg_in[0, k, 0], msg_in[1, k, 0])
        for f in range(4):
            surf[1, f, 16 * k : 16 * k + 16, :] = unpack_edge(packed, RIM, f)
        packed = jnp.where(left_t, msg_in[0, k, 1], msg_in[1, k, 1])
        rows, at = ((slice(8, 16), 0), (slice(0, 16), 8), (slice(0, 8), 24))[k]
        packed = packed[rows]
        for c in range(LEV):
            trac[1, c, at : at + packed.shape[0], :] = unpack_edge(packed, TRIM, c)

    for_lat(wait_forward)

    @pl.when(lat == top)
    def _():
        select = mirror_matrix()
        for k in range(1, nlon):
            fold_arrivals(k)[0].wait_recv()
        ghost = permute_columns(mirrored(fold_surf), select)
        for f in range(4):
            rows = ghost[RIM * f : RIM * f + RIM]
            rows = -rows if f in (1, 2) else rows
            for tile in range(2):
                surf[tile, f, 32 : 32 + RIM, :] = rows[:, LANES * tile : LANES * tile + LANES]
        for k in range(1, nlon):
            fold_arrivals(k)[1].wait_recv()
        ghost = permute_columns(mirrored(fold_trac), select)
        for c in range(LEV):
            rows = ghost[TRIM * c : TRIM * c + TRIM]
            for tile in range(2):
                trac[tile, c, 24 : 24 + TRIM, :] = rows[:, LANES * tile : LANES * tile + LANES]

    h, e, n, wet = (tuple(surf[tile, f] for tile in range(2)) for f in range(4))
    for _ in range(SUB):
        h, e, n = step_forward(h, e, n, wet)
    new_e, new_n = e[0][16:32], n[0][16:32]

    for tile in range(2):
        for c in range(LEV):
            inputs[tile, 32 * c : 32 * c + 32, :] = trac[tile, c]
        inputs[tile, 32 * HCH : 32 * HCH + 32, :] = h[tile][8:40]
    for row in range(22):
        store_shifted(xs1, row, tuple(inputs[tile, pl.ds(5 + row, 16, stride=32), :] for tile in range(2)))
    for row in range(20):
        act = lift(jnp.tanh)(conv_row(weight1, xs1, row))
        for tile in range(2):
            act1[tile, row] = act[tile]
        store_shifted(xs2, row, act)
    for row in range(18):
        act = lift(jnp.tanh)(conv_row(weight2, xs2, row))
        for tile in range(2):
            act2[tile, row] = act[tile]
        store_shifted(xs3, row, act)

    def weight_sum(gs, xs, rows):
        total = jnp.zeros((16, 144), F32)
        for row in range(rows):
            grad = jnp.concatenate([gs[tile, row + 2, 16:32, :] for tile in range(2)], axis=1)
            total = total + contract(grad, patch(xs, row))
        return total

    def back_layer(weight, gs, act_ref, out, rows):
        for row in range(rows):
            grad = conv_row(weight, gs, row)
            act = tuple(act_ref[tile, row] for tile in range(2))
            store_shifted(out, row + 2, lift(lambda g, a: g * (1.0 - a * a))(grad, act))

    sum3 = weight_sum(gs3, xs3, 16)
    back_layer(flip3, gs3, act2, gs2, 18)
    sum2 = weight_sum(gs2, xs2, 18)
    back_layer(flip2, gs2, act1, gs1, 20)
    sum1 = weight_sum(gs1, xs1, 20)

    tail = jnp.concatenate([sum1[:, 128:144], sum2[:, 128:144], sum3[:, 128:144], jnp.zeros((16, 80), F32)], axis=1)
    rows = jnp.concatenate([sum1[:, :128], sum2[:, :128], sum3[:, :128], tail], axis=0)
    for k in range(nlon):
        wsum[k] = rows[chunk * k : chunk * k + chunk]

    def scatter_copy(k):
        peer = lax.rem(lon + k, nlon)
        return remote(wsum.at[peer], rs_in.at[k], ar_send.at[0, k], ar_recv.at[0, k], lon=peer)

    def part_copy(k):
        other = lax.rem(place + k, group)
        return remote(
            part_in.at[place],
            part_in.at[place],
            ar_send.at[1, k],
            ar_recv.at[1, k],
            lat=lax.rem(other, nlat),
            ens=other // nlat,
        )

    def part_arrival(k):
        other = lax.rem(place + group - k, group)
        return remote(
            part_in.at[place],
            part_in.at[other],
            ar_send.at[1, k],
            ar_recv.at[1, k],
            lat=lax.rem(other, nlat),
            ens=other // nlat,
        )

    def full_copy(k):
        peer = lax.rem(lon + k, nlon)
        return remote(full.at[lon], full.at[lon], ar_send.at[2, k], ar_recv.at[2, k], lon=peer)

    def full_arrival(k):
        source = lax.rem(lon + nlon - k, nlon)
        return remote(full.at[lon], full.at[source], ar_send.at[2, k], ar_recv.at[2, k], lon=source)

    for k in range(1, nlon):
        scatter_copy(k).start()

    for row in range(22):
        grad = conv_row(flip1, gs1, row)
        for tile in range(2):
            back[tile, pl.ds(5 + row, 16, stride=32), :] = grad[tile]

    lane16 = lane_iota(16)
    zero8 = jnp.zeros((8, LANES), F32)
    sum_e = jnp.zeros((16, LANES), F32)
    sum_n = jnp.zeros((16, LANES), F32)
    for c in range(LEV):
        bar = bar_t[c]
        wb = wet_own * bar
        own, halo = trac[0, c, 8:24, :], trac[1, c, 8:24, :]
        ahead = jnp.where(lane16 == LANES - 1, pltpu.roll(halo, LANES - 1, 1), pltpu.roll(own, LANES - 1, 1))
        behind = jnp.where(lane16 == 0, pltpu.roll(halo, 1, 1), pltpu.roll(own, 1, 1))
        sum_e = sum_e + wb * (ahead - behind)
        sum_n = sum_n + wb * (trac[0, c, 9:25, :] - trac[0, c, 7:23, :])
        qe = (0.5 * advection) * new_e * wb
        qn = (0.5 * advection) * new_n * wb
        wd = diffusion * wb
        up = pltpu.roll(wd + qe, LANES - 1, 1)
        down = pltpu.roll(wd - qe, 1, 1)
        middle = (
            bar - 4.0 * wd + jnp.where(lane16 < LANES - 1, up, 0.0) + jnp.where(lane16 > 0, down, 0.0)
        )
        side = jnp.where(lane16 == LANES - 1, up, jnp.where(lane16 == 0, down, 0.0))
        above = pltpu.roll(jnp.concatenate([zero8, wd + qn, zero8], axis=0), 31, 0)
        below = pltpu.roll(jnp.concatenate([zero8, wd - qn, zero8], axis=0), 1, 0)
        main = jnp.concatenate([zero8, middle, zero8], axis=0) + above + below
        side = jnp.concatenate([zero8, side, zero8], axis=0)
        if c < CL:
            main = main + back[0, 32 * c : 32 * c + 32, :]
            side = side + back[1, 32 * c : 32 * c + 32, :]
        tg[0, c] = main
        tg[1, c] = side

    def own_rows(x):
        zero16 = jnp.zeros((16, LANES), F32)
        return (jnp.concatenate([zero16, x, zero16], axis=0), jnp.zeros((48, LANES), F32))

    e = own_rows(bar_f[0] - (0.5 * advection) * sum_e)
    n = own_rows(bar_f[1] - (0.5 * advection) * sum_n)
    rim = tuple(jnp.concatenate([zero8, back[tile, 32 * HCH : 32 * HCH + 32, :], zero8], axis=0) for tile in range(2))
    h = lift(lambda a, b: a + b)(rim, own_rows(bar_h[...]))
    wet = tuple(surf[tile, 3] for tile in range(2))
    for index in range(SUB):
        h, e, n = step_adjoint(h, e, n, wet)
        if index == 1:
            for k in range(1, nlon):
                scatter_copy(k).wait_recv()
            part = wsum[lon]
            for k in range(1, nlon):
                part = part + rs_in[k]
            part_in[place] = part
            for k in range(1, group):
                part_copy(k).start()
    for f, pair in enumerate((h, e, n)):
        for tile in range(2):
            sg[tile, f] = pair[tile]

    for block in range(3):
        back_out[block, 0] = pack_edges([sg[1, f, 16 * block : 16 * block + 16, :] for f in range(3)], RIM)
        if block == 1:
            fields = [tg[1, c, 8:24, :] for c in range(LEV)]
        elif block == 0:
            fields = [jnp.concatenate([zero8, tg[1, c, 0:8, :]], axis=0) for c in range(LEV)]
        else:
            fields = [jnp.concatenate([tg[1, c, 24:32, :], zero8], axis=0) for c in range(LEV)]
        back_out[block, 1] = pack_edges(fields, TRIM)

    def lat_back(up):
        to = 1 if up else -1
        rows_s = slice(32, 48) if up else slice(0, 16)
        rows_t = slice(24, 32) if up else slice(0, 8)
        slot = 0 if up else 1
        return (
            remote(sg.at[0, :, rows_s, :], back_surf.at[slot], b_send.at[0, slot], b_recv.at[0, slot], lat=lat + to),
            remote(tg.at[0, :, rows_t, :], back_trac.at[slot], b_send.at[1, slot], b_recv.at[1, slot], lat=lat + to),
        )

    def edge_back(side, block, same=False):
        slot = 3 if same else 2 - block
        to = lat if same else lat + block - 1
        return remote(
            back_out.at[block],
            back_in.at[side, slot],
            bm_send.at[side, slot],
            bm_recv.at[side, slot],
            lon=(right, left)[side],
            lat=to,
        )

    @pl.when(lat == top)
    def _():
        for side in range(2):
            edge_back(side, 2, True).start()

    def start_back(shift):
        if shift:
            for copy in lat_back(shift > 0):
                copy.start()
        for side in range(2):
            edge_back(side, shift + 1).start()

    for_lat(start_back)

    right_s = slot_mask(16, RIM, 3, RIM)
    right_t = slot_mask(16, TRIM, LEV, TRIM)

    def unfold_copies(k):
        peer = lax.rem(lon + k, nlon)
        return (
            remote(unfold_surf.at[lon], unfold_surf.at[lon], unfold_send.at[0, k], unfold_recv.at[0, k], lon=peer),
            remote(unfold_trac.at[lon], unfold_trac.at[lon], unfold_send.at[1, k], unfold_recv.at[1, k], lon=peer),
        )

    def unfold_arrivals(k):
        source = lax.rem(lon + nlon - k, nlon)
        return (
            remote(unfold_surf.at[lon], unfold_surf.at[source], unfold_send.at[0, k], unfold_recv.at[0, k], lon=source),
            remote(unfold_trac.at[lon], unfold_trac.at[source], unfold_send.at[1, k], unfold_recv.at[1, k], lon=source),
        )

    @pl.when(lat == top)
    def _():
        for side in range(2):
            edge_back(side, 2, True).wait_recv()
        packed = jnp.where(right_s, back_in[0, 3, 0], back_in[1, 3, 0])
        for f in range(3):
            sg[0, f, 32:48, :] = sg[0, f, 32:48, :] + unpack_edge(packed, RIM, f)
            for j in range(RIM):
                row = RIM * f + j
                unfold_surf[lon, row : row + 1, :] = sg[0, f, 42 - j : 43 - j, :]
        packed = jnp.where(right_t, back_in[0, 3, 1], back_in[1, 3, 1])[0:8]
        for c in range(LEV):
            tg[0, c, 24:32, :] = tg[0, c, 24:32, :] + unpack_edge(packed, TRIM, c)
            for j in range(TRIM):
                row = TRIM * c + j
                unfold_trac[lon, row : row + 1, :] = tg[0, c, 26 - j : 27 - j, :]
        for k in range(1, nlon):
            for copy in unfold_copies(k):
                copy.start()

    for k in range(1, group):
        part_arrival(k).wait_recv()
    total = part_in[0]
    for k in range(1, group):
        total = total + part_in[k]
    full[lon] = total
    for k in range(1, nlon):
        full_copy(k).start()

    def wait_back(shift):
        if shift:
            for copy in lat_back(shift < 0):
                copy.wait_recv()
        for side in range(2):
            edge_back(side, 1 - shift).wait_recv()

    for_lat(wait_back)

    from_left = back_in[0, 0] + back_in[0, 1] + back_in[0, 2]
    from_right = back_in[1, 0] + back_in[1, 1] + back_in[1, 2]
    packed = jnp.where(right_s, from_left[0], from_right[0])
    for f in range(3):
        total = sg[0, f, 16:32, :] + back_surf[0, f] + back_surf[1, f] + unpack_edge(packed, RIM, f)
        if f == 0:
            height_out[0] = total
        else:
            flow_out[0, f - 1] = total
    packed = jnp.where(right_t, from_left[1], from_right[1])
    for c in range(LEV):
        ghosts = jnp.concatenate([back_trac[0, c], back_trac[1, c]], axis=0)
        temp_out[0, c] = tg[0, c, 8:24, :] + ghosts + unpack_edge(packed, TRIM, c)

    for k in range(1, nlon):
        full_arrival(k).wait_recv()
    scale = 1.0 / math.sqrt(nens * nlat * 16 * nlon * LANES)
    rows = jnp.concatenate([full[k] for k in range(nlon)], axis=0) * scale
    for layer, out in ((1, second_out), (2, third_out)):
        count = out.shape[0]
        out[:, 0:128] = rows[16 * layer : 16 * layer + count]
        out[:, 128:144] = rows[48 : 48 + count, 16 * layer : 16 * layer + 16]
    for tap in range(9):
        block = rows[48:64, 0:16] if tap == 8 else rows[0:16, 16 * tap : 16 * tap + 16]
        first_out[:, 11 * tap : 11 * tap + CL] = block[:, 0:CL]
        first_out[:, 11 * tap + CL : 11 * tap + CL + 1] = block[:, HCH : HCH + 1]

    @pl.when(lat == top)
    def _():
        for k in range(1, nlon):
            for copy in unfold_arrivals(k):
                copy.wait_recv()
        source = lax.broadcasted_iota(jnp.int32, (3 * LANES, LANES), 0)
        column = lax.broadcasted_iota(jnp.int32, (3 * LANES, LANES), 1)
        select = jnp.where(source + column == offset, 1.0, 0.0).astype(BF16)
        ghost = permute_columns(mirrored(unfold_surf), select)
        height_out[0, 16 - RIM : 16, :] = height_out[0, 16 - RIM : 16, :] + ghost[0:RIM]
        for f in (1, 2):
            flow_out[0, f - 1, 16 - RIM : 16, :] = (
                flow_out[0, f - 1, 16 - RIM : 16, :] - ghost[RIM * f : RIM * f + RIM]
            )
        ghost = permute_columns(mirrored(unfold_trac), select)
        for c in range(LEV):
            temp_out[0, c, 16 - TRIM : 16, :] = (
                temp_out[0, c, 16 - TRIM : 16, :] + ghost[TRIM * c : TRIM * c + TRIM]
            )

    def sent_forward(shift):
        if shift:
            for copy in lat_copies(shift > 0):
                copy.wait_send()
            for copy in lat_back(shift > 0):
                copy.wait_send()
        for side in range(2):
            edge_copy(side, shift).wait_send()
            edge_back(side, shift + 1).wait_send()

    for_lat(sent_forward)
    for k in range(1, nlon):
        scatter_copy(k).wait_send()
        full_copy(k).wait_send()
    for k in range(1, group):
        part_copy(k).wait_send()

    @pl.when(lat == top)
    def _():
        for side in range(2):
            edge_back(side, 2, True).wait_send()
        for k in range(1, nlon):
            for copy in fold_copies(k) + unfold_copies(k):
                copy.wait_send()


def solution(mesh):
    nlon, nlat, nens = (mesh.shape[axis] for axis in ("lon", "lat", "ens"))
    group = nlat * nens

    def local(temp, height, flow, land_sea, fold, w_first, w_second, w_third, temp_bar, height_bar, flow_bar):
        vmem = pltpu.VMEM
        dma = pltpu.SemaphoreType.DMA
        chunk = 64 // nlon
        scratch = [
            vmem((2, 4, 48, LANES), F32),
            vmem((2, LEV, 32, LANES), F32),
            vmem((2, 16 * 32, LANES), F32),
            vmem((16, LANES), jnp.int32),
            vmem((LEV, 16, LANES), F32),
            vmem((16, LANES), F32),
            vmem((2, 16, LANES), F32),
            pltpu.SMEM(fold.shape, jnp.int32),
            vmem(w_first.shape, BF16),
            vmem(w_second.shape, BF16),
            vmem(w_third.shape, BF16),
            vmem((3, 16, 256), F32),
            vmem((3, 16, 144), F32),
            vmem((2, 16, LANES), F32),
            vmem((2, 3, 2, 16, LANES), F32),
            vmem((nlon, 48, LANES), F32),
            vmem((nlon, 40, LANES), F32),
            vmem((16 * 16, LANES), F32),
            vmem((2, 22, 48, LANES), BF16),
            vmem((2, 20, 48, LANES), BF16),
            vmem((2, 18, 48, LANES), BF16),
            vmem((2, 24, 48, LANES), BF16),
            vmem((2, 22, 48, LANES), BF16),
            vmem((2, 20, 48, LANES), BF16),
            vmem((2, 20, 16, LANES), F32),
            vmem((2, 18, 16, LANES), F32),
            vmem((2, 16 * 32, LANES), F32),
            vmem((2, 3, 48, LANES), F32),
            vmem((2, LEV, 32, LANES), F32),
            vmem((3, 2, 16, LANES), F32),
            vmem((2, 4, 2, 16, LANES), F32),
            vmem((2, 3, 16, LANES), F32),
            vmem((2, LEV, 8, LANES), F32),
            vmem((nlon, 40, LANES), F32),
            vmem((nlon, 40, LANES), F32),
            vmem((nlon, chunk, LANES), F32),
            vmem((nlon, chunk, LANES), F32),
            vmem((group, chunk, LANES), F32),
            vmem((nlon, chunk, LANES), F32),
            dma((11,)),
            dma((4,)),
            dma((4,)),
            dma((6,)),
            dma((6,)),
            dma((2, nlon)),
            dma((2, nlon)),
            dma((2, 2)),
            dma((2, 2)),
            dma((2, 4)),
            dma((2, 4)),
            dma((2, nlon)),
            dma((2, nlon)),
            dma((3, max(nlon, group))),
            dma((3, max(nlon, group))),
        ]
        out_shape = (
            jax.ShapeDtypeStruct(temp.shape, F32),
            jax.ShapeDtypeStruct(height.shape, F32),
            jax.ShapeDtypeStruct(flow.shape, F32),
            jax.ShapeDtypeStruct(w_first.shape, F32),
            jax.ShapeDtypeStruct(w_second.shape, F32),
            jax.ShapeDtypeStruct(w_third.shape, F32),
        )
        return pl.pallas_call(
            functools.partial(kernel, (nlon, nlat, nens)),
            out_shape=out_shape,
            in_specs=[pl.BlockSpec(memory_space=pl.ANY)] * 11,
            out_specs=[pl.BlockSpec(memory_space=pltpu.VMEM)] * 6,
            scratch_shapes=scratch,
            compiler_params=pltpu.CompilerParams(
                collective_id=0, has_side_effects=True, vmem_limit_bytes=32 * 1024 * 1024
            ),
        )(temp, height, flow, land_sea, fold, w_first, w_second, w_third, temp_bar, height_bar, flow_bar)

    field = P("ens", None, "lat", "lon")
    plane = P("ens", "lat", "lon")
    return jax.shard_map(
        local,
        mesh=mesh,
        in_specs=(field, plane, field, P("lat", "lon"), P(), P(), P(), P(), field, plane, field),
        out_specs=(field, plane, field, P(), P(), P()),
        check_vma=False,
    )
```

time: 799 us -> 57.2 us (0.07)
  the two profiles are of different devices: /device:TPU:1 before, /device:TPU:29 now
where the time goes in v1:
time: 57.2 us; the launch traced here: 56.5 us
  Pallas kernels  44.1 us (77%)
  local copies, waits for them, and re-layouts  11.7 us (20%)
  between operations  0.67 us (1%)
    pallas_call x1, Pallas kernels, local(): pl.pallas_call(functools.partial(kernel, (nlon, nlat, nens)), out_shape=o...  44.1 us
    unnamed x28, local copies, waits for them, and re-layouts  11.7 us

profile of v1, /device:TPU:29, one launch (start us, length us, event | category | flops | bytes accessed | tf_op | source)
XLA Modules:
  0.0 56.5 jit_solution(15540108641326734701)
XLA Ops:
  0.6 0.0 copy-start
  0.6 0.9 %copy-done = f32[1,12,16,128]{3,2,1,0:T(8,128)S(1)} copy-done((f32[1,12,16,128]{3,2,1,0:T(8,128)S(1)}, f32[1,12,16,128]{3,2,1,0:T(8,128)}, u32[]{:S(2)}) %copy-start) | copy-done | bytes 98328
  1.5 0.0 copy-start.1
  1.5 0.9 %copy-done.1 = f32[1,12,16,128]{3,2,1,0:T(8,128)S(1)} copy-done((f32[1,12,16,128]{3,2,1,0:T(8,128)S(1)}, f32[1,12,16,128]{3,2,1,0:T(8,128)}, u32[]{:S(2)}) %copy-start.1) | copy-done | bytes 98328
  2.4 0.0 copy-start.2
  2.4 0.7 %copy-done.2 = f32[1,2,16,128]{3,2,1,0:T(8,128)S(1)} copy-done((f32[1,2,16,128]{3,2,1,0:T(8,128)S(1)}, f32[1,2,16,128]{3,2,1,0:T(8,128)}, u32[]{:S(2)}) %copy-start.2) | copy-done | bytes 16408
  3.1 0.0 copy-start.3
  3.1 0.7 %copy-done.3 = f32[1,2,16,128]{3,2,1,0:T(8,128)S(1)} copy-done((f32[1,2,16,128]{3,2,1,0:T(8,128)S(1)}, f32[1,2,16,128]{3,2,1,0:T(8,128)}, u32[]{:S(2)}) %copy-start.3) | copy-done | bytes 16408
  3.9 0.0 copy-start.4
  3.9 0.7 %copy-done.4 = f32[1,16,128]{2,1,0:T(8,128)S(1)} copy-done((f32[1,16,128]{2,1,0:T(8,128)S(1)}, f32[1,16,128]{2,1,0:T(8,128)}, u32[]{:S(2)}) %copy-start.4) | copy-done | bytes 8216
  4.6 0.0 copy-start.5
  4.6 0.7 %copy-done.5 = s32[16,128]{1,0:T(8,128)S(1)} copy-done((s32[16,128]{1,0:T(8,128)S(1)}, s32[16,128]{1,0:T(8,128)}, u32[]{:S(2)}) %copy-start.5) | copy-done | bytes 8216
  5.3 0.0 copy-start.6
  5.3 0.7 %copy-done.6 = s32[2048]{0:T(1024)S(1)} copy-done((s32[2048]{0:T(1024)S(1)}, s32[2048]{0:T(1024)}, u32[]{:S(2)}) %copy-start.6) | copy-done | bytes 8216
  6.0 0.0 copy-start.7
  6.0 0.7 %copy-done.7 = bf16[16,144]{1,0:T(8,128)(2,1)S(1)} copy-done((bf16[16,144]{1,0:T(8,128)(2,1)S(1)}, bf16[16,144]{1,0:T(8,128)(2,1)}, u32[]{:S(2)}) %copy-start.7) | copy-done | bytes 4632
  6.6 0.0 copy-start.8
  6.7 0.7 %copy-done.8 = bf16[10,144]{1,0:T(8,128)(2,1)S(1)} copy-done((bf16[10,144]{1,0:T(8,128)(2,1)S(1)}, bf16[10,144]{1,0:T(8,128)(2,1)}, u32[]{:S(2)}) %copy-start.8) | copy-done | bytes 2904
  7.3 0.0 copy-start.9
  7.3 0.7 %copy-done.9 = f32[1,16,128]{2,1,0:T(8,128)S(1)} copy-done((f32[1,16,128]{2,1,0:T(8,128)S(1)}, f32[1,16,128]{2,1,0:T(8,128)}, u32[]{:S(2)}) %copy-start.9) | copy-done | bytes 8216
  8.0 0.0 copy-start.10
  8.0 0.7 %copy-done.10 = bf16[16,99]{1,0:T(8,128)(2,1)S(1)} copy-done((bf16[16,99]{1,0:T(8,128)(2,1)S(1)}, bf16[16,99]{1,0:T(8,128)(2,1)}, u32[]{:S(2)}) %copy-start.10) | copy-done | bytes 3192
  8.7 44.1 %shard_map.154 = (f32[1,12,16,128]{3,2,1,0:T(8,128)S(1)}, f32[1,16,128]{2,1,0:T(8,128)S(1)}, f32[1,2,16,128]{3,2,1,0:T(8,128)S(1)}, f32[16,99]{1,0:T(8,128)S(1)}...) custom-call(f32[1,12,16,128]{3,2,1,0:T(8,128)S(1)} %copy-done, f32[1,16,128]{2,1,0:T(8,128)S(1)} %copy-done.4, ...), custom_call_target="tpu_custom_call" | custom-call | tf_op jit(solution)/shard_map/pallas_call | solution.py:850
  52.8 0.6 %copy.23 = f32[1,12,16,128]{3,2,1,0:T(8,128)} copy(f32[1,12,16,128]{3,2,1,0:T(8,128)S(1)} %get-tuple-element.12) | data formatting | bytes 196608
  53.5 0.6 %copy.24 = f32[1,16,128]{2,1,0:T(8,128)} copy(f32[1,16,128]{2,1,0:T(8,128)S(1)} %get-tuple-element.13) | data formatting | bytes 16384
  54.1 0.6 %copy.25 = f32[1,2,16,128]{3,2,1,0:T(8,128)} copy(f32[1,2,16,128]{3,2,1,0:T(8,128)S(1)} %get-tuple-element.14) | data formatting | bytes 32768
  54.7 0.6 %copy.26 = f32[16,99]{1,0:T(8,128)} copy(f32[16,99]{1,0:T(8,128)S(1)} %get-tuple-element.15) | data formatting | bytes 12672
  55.3 0.6 %copy.27 = f32[16,144]{1,0:T(8,128)} copy(f32[16,144]{1,0:T(8,128)S(1)} %get-tuple-element.16) | data formatting | bytes 18432
  55.9 0.6 %copy.28 = f32[10,144]{1,0:T(8,128)} copy(f32[10,144]{1,0:T(8,128)S(1)} %get-tuple-element.17) | data formatting | bytes 11520
Async XLA Ops:
  0.6 0.9 %copy-start = (f32[1,12,16,128]{3,2,1,0:T(8,128)S(1)}, f32[1,12,16,128]{3,2,1,0:T(8,128)}, u32[]{:S(2)}) copy-start(f32[1,12,16,128]{3,2,1,0:T(8,128)} %temp.1) | copy-start | bytes 294916
  1.5 0.9 %copy-start.1 = (f32[1,12,16,128]{3,2,1,0:T(8,128)S(1)}, f32[1,12,16,128]{3,2,1,0:T(8,128)}, u32[]{:S(2)}) copy-start(f32[1,12,16,128]{3,2,1,0:T(8,128)} %temp_bar.1) | copy-start | bytes 294916
  2.4 0.7 %copy-start.2 = (f32[1,2,16,128]{3,2,1,0:T(8,128)S(1)}, f32[1,2,16,128]{3,2,1,0:T(8,128)}, u32[]{:S(2)}) copy-start(f32[1,2,16,128]{3,2,1,0:T(8,128)} %flow.1) | copy-start | bytes 49156
  3.1 0.7 %copy-start.3 = (f32[1,2,16,128]{3,2,1,0:T(8,128)S(1)}, f32[1,2,16,128]{3,2,1,0:T(8,128)}, u32[]{:S(2)}) copy-start(f32[1,2,16,128]{3,2,1,0:T(8,128)} %flow_bar.1) | copy-start | bytes 49156
  3.9 0.7 %copy-start.4 = (f32[1,16,128]{2,1,0:T(8,128)S(1)}, f32[1,16,128]{2,1,0:T(8,128)}, u32[]{:S(2)}) copy-start(f32[1,16,128]{2,1,0:T(8,128)} %height.1) | copy-start | bytes 24580
  4.6 0.7 %copy-start.5 = (s32[16,128]{1,0:T(8,128)S(1)}, s32[16,128]{1,0:T(8,128)}, u32[]{:S(2)}) copy-start(s32[16,128]{1,0:T(8,128)} %land_sea.1) | copy-start | bytes 24580
  5.3 0.7 %copy-start.6 = (s32[2048]{0:T(1024)S(1)}, s32[2048]{0:T(1024)}, u32[]{:S(2)}) copy-start(s32[2048]{0:T(1024)} %fold.1) | copy-start | bytes 24580
  6.0 0.7 %copy-start.7 = (bf16[16,144]{1,0:T(8,128)(2,1)S(1)}, bf16[16,144]{1,0:T(8,128)(2,1)}, u32[]{:S(2)}) copy-start(bf16[16,144]{1,0:T(8,128)(2,1)} %w_second.1) | copy-start | bytes 13828
  6.6 0.7 %copy-start.8 = (bf16[10,144]{1,0:T(8,128)(2,1)S(1)}, bf16[10,144]{1,0:T(8,128)(2,1)}, u32[]{:S(2)}) copy-start(bf16[10,144]{1,0:T(8,128)(2,1)} %w_third.1) | copy-start | bytes 8644
  7.3 0.7 %copy-start.9 = (f32[1,16,128]{2,1,0:T(8,128)S(1)}, f32[1,16,128]{2,1,0:T(8,128)}, u32[]{:S(2)}) copy-start(f32[1,16,128]{2,1,0:T(8,128)} %height_bar.1) | copy-start | bytes 24580
  8.0 0.7 %copy-start.10 = (bf16[16,99]{1,0:T(8,128)(2,1)S(1)}, bf16[16,99]{1,0:T(8,128)(2,1)}, u32[]{:S(2)}) copy-start(bf16[16,99]{1,0:T(8,128)(2,1)} %w_first.1) | copy-start | bytes 9508

commit v2 on v1

--- a/solution.py
+++ b/solution.py
@@ -198,10 +198,12 @@
     back_trac,
     unfold_surf,
     unfold_trac,
-    wsum,
-    rs_in,
-    part_in,
-    full,
+    unfold_edge,
+    halves,
+    half_in,
+    plane_in,
+    column_in,
+    totals,
     load_sem,
     f_send,
     f_recv,
@@ -215,16 +217,21 @@
     bm_recv,
     unfold_send,
     unfold_recv,
-    ar_send,
-    ar_recv,
+    pair_send,
+    pair_recv,
+    plane_send,
+    plane_recv,
+    column_send,
+    column_recv,
 ):
     nlon, nlat, nens = sizes
     lon, lat, ens = lax.axis_index("lon"), lax.axis_index("lat"), lax.axis_index("ens")
     top = nlat - 1
     left, right = lax.rem(lon + nlon - 1, nlon), lax.rem(lon + 1, nlon)
-    group = nlat * nens
-    place = ens * nlat + lat
-    chunk = 64 // nlon
+    nz, ny = nlon // 2, nlat // 2
+    core, z = lax.rem(lat, 2), lax.rem(lon, nz)
+    plane = 2 * ny * nens
+    place = (ens * 2 + lon // nz) * ny + lat // 2
 
     def remote(src, dst, send, recv, **device):
         return pltpu.make_async_remote_copy(
@@ -236,21 +243,35 @@
     def greet(**device):
         pl.semaphore_signal(barrier, inc=1, device_id=device, device_id_type=MESH)
 
-    for k in range(1, nlon):
-        greet(lon=lax.rem(lon + k, nlon))
-    for k in range(1, group):
-        other = lax.rem(place + k, group)
-        greet(lat=lax.rem(other, nlat), ens=other // nlat)
+    def plane_device(index):
+        return dict(lon=lax.rem(index // ny, 2) * nz + z, lat=lax.rem(index, ny) * 2 + core, ens=index // (2 * ny))
+
+    def column_device(index):
+        return dict(lon=(lon // nz) * nz + index)
+
+    for k in range(1, plane):
+        greet(**plane_device(lax.rem(place + k, plane)))
+    for k in range(1, nz):
+        greet(**column_device(lax.rem(z + k, nz)))
+    greet(lon=left)
+    greet(lon=right)
 
     @pl.when(lat > 0)
     def _():
+        greet(lat=lat - 1)
         greet(lon=left, lat=lat - 1)
         greet(lon=right, lat=lat - 1)
 
     @pl.when(lat < top)
     def _():
+        greet(lat=lat + 1)
         greet(lon=left, lat=lat + 1)
         greet(lon=right, lat=lat + 1)
+
+    @pl.when(lat == top)
+    def _():
+        for k in range(1, nlon):
+            greet(lon=lax.rem(lon + k, nlon))
 
     loads = [
         (temp.at[0], trac.at[0, :, 8:24, :]),
@@ -277,8 +298,9 @@
     back[...] = jnp.zeros_like(back)
     fold_surf[lon, 40:48, :] = jnp.zeros((8, LANES), F32)
     fold_trac[lon, 32:40, :] = jnp.zeros((8, LANES), F32)
-    unfold_surf[lon, 32:40, :] = jnp.zeros((8, LANES), F32)
-    unfold_trac[lon, 32:40, :] = jnp.zeros((8, LANES), F32)
+    for ref in (unfold_surf, unfold_trac):
+        ref[lon, 32:40, :] = jnp.zeros((8, LANES), F32)
+    unfold_edge[:, 32:40, :] = jnp.zeros((2, 8, LANES), F32)
 
     @pl.when(lat == 0)
     def _():
@@ -350,7 +372,13 @@
                 fold_trac[lon, row : row + 1, :] = trac[0, c, 23 - m : 24 - m, :]
 
     pl.semaphore_wait(
-        barrier, (nlon - 1) + (group - 1) + 2 * (lat > 0).astype(jnp.int32) + 2 * (lat < top).astype(jnp.int32)
+        barrier,
+        (plane - 1)
+        + (nz - 1)
+        + 2
+        + 3 * (lat > 0).astype(jnp.int32)
+        + 3 * (lat < top).astype(jnp.int32)
+        + (nlon - 1) * (lat == top).astype(jnp.int32),
     )
 
     def for_lat(fn):
@@ -450,6 +478,15 @@
             rows = -rows if f in (1, 2) else rows
             for tile in range(2):
                 surf[tile, f, 32 : 32 + RIM, :] = rows[:, LANES * tile : LANES * tile + LANES]
+
+    h, e, n, wet = (tuple(surf[tile, f] for tile in range(2)) for f in range(4))
+    for _ in range(SUB):
+        h, e, n = step_forward(h, e, n, wet)
+    new_e, new_n = e[0][16:32], n[0][16:32]
+
+    @pl.when(lat == top)
+    def _():
+        select = mirror_matrix()
         for k in range(1, nlon):
             fold_arrivals(k)[1].wait_recv()
         ghost = permute_columns(mirrored(fold_trac), select)
@@ -458,10 +495,6 @@
             for tile in range(2):
                 trac[tile, c, 24 : 24 + TRIM, :] = rows[:, LANES * tile : LANES * tile + LANES]
 
-    h, e, n, wet = (tuple(surf[tile, f] for tile in range(2)) for f in range(4))
-    for _ in range(SUB):
-        h, e, n = step_forward(h, e, n, wet)
-    new_e, new_n = e[0][16:32], n[0][16:32]
 
     for tile in range(2):
         for c in range(LEV):
@@ -500,46 +533,39 @@
     sum1 = weight_sum(gs1, xs1, 20)
 
     tail = jnp.concatenate([sum1[:, 128:144], sum2[:, 128:144], sum3[:, 128:144], jnp.zeros((16, 80), F32)], axis=1)
-    rows = jnp.concatenate([sum1[:, :128], sum2[:, :128], sum3[:, :128], tail], axis=0)
-    for k in range(nlon):
-        wsum[k] = rows[chunk * k : chunk * k + chunk]
-
-    def scatter_copy(k):
-        peer = lax.rem(lon + k, nlon)
-        return remote(wsum.at[peer], rs_in.at[k], ar_send.at[0, k], ar_recv.at[0, k], lon=peer)
-
-    def part_copy(k):
-        other = lax.rem(place + k, group)
+    tail = jnp.concatenate([tail[0:6, 0:48], tail[6:12, 0:48], tail[10:16, 0:32]], axis=1)
+    rows = jnp.concatenate([sum1[:, :128], sum2[:, :128], sum3[0:CL, :128], tail], axis=0)
+    halves[0] = rows[0:24]
+    halves[1] = rows[24:48]
+
+    def half_copy():
+        return remote(halves.at[1 - core], half_in, pair_send.at[0], pair_recv.at[0], lat=lat + 1 - 2 * core)
+
+    def plane_copy(k, arrival=False):
+        other = lax.rem(place + (plane - k if arrival else k), plane)
+        slot = other if arrival else place
         return remote(
-            part_in.at[place],
-            part_in.at[place],
-            ar_send.at[1, k],
-            ar_recv.at[1, k],
-            lat=lax.rem(other, nlat),
-            ens=other // nlat,
-        )
-
-    def part_arrival(k):
-        other = lax.rem(place + group - k, group)
+            plane_in.at[place], plane_in.at[slot], plane_send.at[k], plane_recv.at[k], **plane_device(other)
+        )
+
+    def column_copy(k, arrival=False):
+        other = lax.rem(z + (nz - k if arrival else k), nz)
+        slot = other if arrival else z
         return remote(
-            part_in.at[place],
-            part_in.at[other],
-            ar_send.at[1, k],
-            ar_recv.at[1, k],
-            lat=lax.rem(other, nlat),
-            ens=other // nlat,
-        )
-
-    def full_copy(k):
-        peer = lax.rem(lon + k, nlon)
-        return remote(full.at[lon], full.at[lon], ar_send.at[2, k], ar_recv.at[2, k], lon=peer)
-
-    def full_arrival(k):
-        source = lax.rem(lon + nlon - k, nlon)
-        return remote(full.at[lon], full.at[source], ar_send.at[2, k], ar_recv.at[2, k], lon=source)
-
-    for k in range(1, nlon):
-        scatter_copy(k).start()
+            column_in.at[z], column_in.at[slot], column_send.at[k], column_recv.at[k], **column_device(other)
+        )
+
+    def total_copy(arrival=False):
+        slot = 1 - core if arrival else core
+        return remote(totals.at[core], totals.at[slot], pair_send.at[1], pair_recv.at[1], lat=lat + 1 - 2 * core)
+
+    def sum_slots(ref, count):
+        total = ref[0]
+        for k in range(1, count):
+            total = total + ref[k]
+        return total
+
+    half_copy().start()
 
     for row in range(22):
         grad = conv_row(flip1, gs1, row)
@@ -577,6 +603,52 @@
         tg[0, c] = main
         tg[1, c] = side
 
+    def lat_back(up):
+        to = 1 if up else -1
+        rows_s = slice(32, 48) if up else slice(0, 16)
+        rows_t = slice(24, 32) if up else slice(0, 8)
+        slot = 0 if up else 1
+        return (
+            remote(sg.at[0, :, rows_s, :], back_surf.at[slot], b_send.at[0, slot], b_recv.at[0, slot], lat=lat + to),
+            remote(tg.at[0, :, rows_t, :], back_trac.at[slot], b_send.at[1, slot], b_recv.at[1, slot], lat=lat + to),
+        )
+
+    def unfold_copies(k):
+        peer = lax.rem(lon + k, nlon)
+        return (
+            remote(unfold_surf.at[lon], unfold_surf.at[lon], unfold_send.at[0, k], unfold_recv.at[0, k], lon=peer),
+            remote(unfold_trac.at[lon], unfold_trac.at[lon], unfold_send.at[1, k], unfold_recv.at[1, k], lon=peer),
+        )
+
+    def unfold_arrivals(k):
+        source = lax.rem(lon + nlon - k, nlon)
+        return (
+            remote(unfold_surf.at[lon], unfold_surf.at[source], unfold_send.at[0, k], unfold_recv.at[0, k], lon=source),
+            remote(unfold_trac.at[lon], unfold_trac.at[source], unfold_send.at[1, k], unfold_recv.at[1, k], lon=source),
+        )
+
+    def pack_ghosts(grads, first, count, width, out, edge):
+        for f in range(count):
+            for j in range(width):
+                row, ghost = width * f + j, first + width - 1 - j
+                out[lon, row : row + 1, :] = grads[0, f, ghost : ghost + 1, :]
+                edge[row : row + 1, :] = grads[1, f, ghost : ghost + 1, :]
+        out[lon, 40:48, :] = pack_edges([edge[8 * g : 8 * g + 8, :] for g in range(5)], width)
+
+    @pl.when(lat == top)
+    def _():
+        pack_ghosts(tg, 24, LEV, TRIM, unfold_trac, unfold_edge.at[0])
+        for k in range(1, nlon):
+            unfold_copies(k)[1].start()
+
+    pl.when(lat > 0)(lambda: lat_back(False)[1].start())
+    pl.when(lat < top)(lambda: lat_back(True)[1].start())
+
+    half_copy().wait_recv()
+    plane_in[place] = halves[core] + half_in[...]
+    for k in range(1, plane):
+        plane_copy(k).start()
+
     def own_rows(x):
         zero16 = jnp.zeros((16, LANES), F32)
         return (jnp.concatenate([zero16, x, zero16], axis=0), jnp.zeros((48, LANES), F32))
@@ -588,15 +660,6 @@
     wet = tuple(surf[tile, 3] for tile in range(2))
     for index in range(SUB):
         h, e, n = step_adjoint(h, e, n, wet)
-        if index == 1:
-            for k in range(1, nlon):
-                scatter_copy(k).wait_recv()
-            part = wsum[lon]
-            for k in range(1, nlon):
-                part = part + rs_in[k]
-            part_in[place] = part
-            for k in range(1, group):
-                part_copy(k).start()
     for f, pair in enumerate((h, e, n)):
         for tile in range(2):
             sg[tile, f] = pair[tile]
@@ -611,37 +674,25 @@
             fields = [jnp.concatenate([tg[1, c, 24:32, :], zero8], axis=0) for c in range(LEV)]
         back_out[block, 1] = pack_edges(fields, TRIM)
 
-    def lat_back(up):
-        to = 1 if up else -1
-        rows_s = slice(32, 48) if up else slice(0, 16)
-        rows_t = slice(24, 32) if up else slice(0, 8)
-        slot = 0 if up else 1
-        return (
-            remote(sg.at[0, :, rows_s, :], back_surf.at[slot], b_send.at[0, slot], b_recv.at[0, slot], lat=lat + to),
-            remote(tg.at[0, :, rows_t, :], back_trac.at[slot], b_send.at[1, slot], b_recv.at[1, slot], lat=lat + to),
-        )
-
-    def edge_back(side, block, same=False):
-        slot = 3 if same else 2 - block
-        to = lat if same else lat + block - 1
+    def edge_back(side, block):
         return remote(
             back_out.at[block],
-            back_in.at[side, slot],
-            bm_send.at[side, slot],
-            bm_recv.at[side, slot],
+            back_in.at[side, 2 - block],
+            bm_send.at[side, 2 - block],
+            bm_recv.at[side, 2 - block],
             lon=(right, left)[side],
-            lat=to,
-        )
-
-    @pl.when(lat == top)
-    def _():
-        for side in range(2):
-            edge_back(side, 2, True).start()
+            lat=lat + block - 1,
+        )
+
+    @pl.when(lat == top)
+    def _():
+        pack_ghosts(sg, 32, 3, RIM, unfold_surf, unfold_edge.at[1])
+        for k in range(1, nlon):
+            unfold_copies(k)[0].start()
 
     def start_back(shift):
         if shift:
-            for copy in lat_back(shift > 0):
-                copy.start()
+            lat_back(shift > 0)[0].start()
         for side in range(2):
             edge_back(side, shift + 1).start()
 
@@ -650,48 +701,11 @@
     right_s = slot_mask(16, RIM, 3, RIM)
     right_t = slot_mask(16, TRIM, LEV, TRIM)
 
-    def unfold_copies(k):
-        peer = lax.rem(lon + k, nlon)
-        return (
-            remote(unfold_surf.at[lon], unfold_surf.at[lon], unfold_send.at[0, k], unfold_recv.at[0, k], lon=peer),
-            remote(unfold_trac.at[lon], unfold_trac.at[lon], unfold_send.at[1, k], unfold_recv.at[1, k], lon=peer),
-        )
-
-    def unfold_arrivals(k):
-        source = lax.rem(lon + nlon - k, nlon)
-        return (
-            remote(unfold_surf.at[lon], unfold_surf.at[source], unfold_send.at[0, k], unfold_recv.at[0, k], lon=source),
-            remote(unfold_trac.at[lon], unfold_trac.at[source], unfold_send.at[1, k], unfold_recv.at[1, k], lon=source),
-        )
-
-    @pl.when(lat == top)
-    def _():
-        for side in range(2):
-            edge_back(side, 2, True).wait_recv()
-        packed = jnp.where(right_s, back_in[0, 3, 0], back_in[1, 3, 0])
-        for f in range(3):
-            sg[0, f, 32:48, :] = sg[0, f, 32:48, :] + unpack_edge(packed, RIM, f)
-            for j in range(RIM):
-                row = RIM * f + j
-                unfold_surf[lon, row : row + 1, :] = sg[0, f, 42 - j : 43 - j, :]
-        packed = jnp.where(right_t, back_in[0, 3, 1], back_in[1, 3, 1])[0:8]
-        for c in range(LEV):
-            tg[0, c, 24:32, :] = tg[0, c, 24:32, :] + unpack_edge(packed, TRIM, c)
-            for j in range(TRIM):
-                row = TRIM * c + j
-                unfold_trac[lon, row : row + 1, :] = tg[0, c, 26 - j : 27 - j, :]
-        for k in range(1, nlon):
-            for copy in unfold_copies(k):
-                copy.start()
-
-    for k in range(1, group):
-        part_arrival(k).wait_recv()
-    total = part_in[0]
-    for k in range(1, group):
-        total = total + part_in[k]
-    full[lon] = total
-    for k in range(1, nlon):
-        full_copy(k).start()
+    for k in range(1, plane):
+        plane_copy(k, True).wait_recv()
+    column_in[z] = sum_slots(plane_in, plane)
+    for k in range(1, nz):
+        column_copy(k).start()
 
     def wait_back(shift):
         if shift:
@@ -716,38 +730,58 @@
         ghosts = jnp.concatenate([back_trac[0, c], back_trac[1, c]], axis=0)
         temp_out[0, c] = tg[0, c, 8:24, :] + ghosts + unpack_edge(packed, TRIM, c)
 
-    for k in range(1, nlon):
-        full_arrival(k).wait_recv()
-    scale = 1.0 / math.sqrt(nens * nlat * 16 * nlon * LANES)
-    rows = jnp.concatenate([full[k] for k in range(nlon)], axis=0) * scale
-    for layer, out in ((1, second_out), (2, third_out)):
-        count = out.shape[0]
-        out[:, 0:128] = rows[16 * layer : 16 * layer + count]
-        out[:, 128:144] = rows[48 : 48 + count, 16 * layer : 16 * layer + 16]
-    for tap in range(9):
-        block = rows[48:64, 0:16] if tap == 8 else rows[0:16, 16 * tap : 16 * tap + 16]
-        first_out[:, 11 * tap : 11 * tap + CL] = block[:, 0:CL]
-        first_out[:, 11 * tap + CL : 11 * tap + CL + 1] = block[:, HCH : HCH + 1]
-
-    @pl.when(lat == top)
-    def _():
+    for k in range(1, nz):
+        column_copy(k, True).wait_recv()
+    totals[core] = sum_slots(column_in, nz)
+    total_copy().start()
+
+    @pl.when(lat == top)
+    def _():
+        lane = lax.broadcasted_iota(jnp.int32, (LANES, LANES), 0)
+        column = lax.broadcasted_iota(jnp.int32, (LANES, LANES), 1)
+        halo = jnp.where(lane < LANES // 2, lane + LANES, lane - LANES)
+        select = jnp.concatenate(
+            [jnp.where(at + LANES * j + column == offset, 1.0, 0.0) for at in (lane, halo) for j in range(3)], axis=0
+        ).astype(BF16)
+
+        def unfold(ref, width):
+            tiles = [ref[lax.rem(tile0 + j, nlon)] for j in range(3)]
+            edges = [
+                jnp.concatenate([unpack_edge(tile[40:48], width, g) for g in range(5)], axis=0) for tile in tiles
+            ]
+            return permute_columns(jnp.concatenate([tile[0:40] for tile in tiles] + edges, axis=1), select)
+
         for k in range(1, nlon):
-            for copy in unfold_arrivals(k):
-                copy.wait_recv()
-        source = lax.broadcasted_iota(jnp.int32, (3 * LANES, LANES), 0)
-        column = lax.broadcasted_iota(jnp.int32, (3 * LANES, LANES), 1)
-        select = jnp.where(source + column == offset, 1.0, 0.0).astype(BF16)
-        ghost = permute_columns(mirrored(unfold_surf), select)
+            unfold_arrivals(k)[1].wait_recv()
+        ghost = unfold(unfold_trac, TRIM)
+        for c in range(LEV):
+            temp_out[0, c, 16 - TRIM : 16, :] = (
+                temp_out[0, c, 16 - TRIM : 16, :] + ghost[TRIM * c : TRIM * c + TRIM]
+            )
+        for k in range(1, nlon):
+            unfold_arrivals(k)[0].wait_recv()
+        ghost = unfold(unfold_surf, RIM)
         height_out[0, 16 - RIM : 16, :] = height_out[0, 16 - RIM : 16, :] + ghost[0:RIM]
         for f in (1, 2):
             flow_out[0, f - 1, 16 - RIM : 16, :] = (
                 flow_out[0, f - 1, 16 - RIM : 16, :] - ghost[RIM * f : RIM * f + RIM]
             )
-        ghost = permute_columns(mirrored(unfold_trac), select)
-        for c in range(LEV):
-            temp_out[0, c, 16 - TRIM : 16, :] = (
-                temp_out[0, c, 16 - TRIM : 16, :] + ghost[TRIM * c : TRIM * c + TRIM]
-            )
+
+    total_copy(True).wait_recv()
+    scale = 1.0 / math.sqrt(nens * nlat * 16 * nlon * LANES)
+    rows = jnp.concatenate([totals[0], totals[1]], axis=0) * scale
+    tail = rows[32 + CL : 48]
+    tail = jnp.concatenate(
+        [tail[:, 0:48], tail[:, 48:96], jnp.concatenate([tail[2:6, 96:128], jnp.zeros((4, 16), F32)], axis=1)], axis=0
+    )
+    for layer, out in ((1, second_out), (2, third_out)):
+        count = out.shape[0]
+        out[:, 0:128] = rows[16 * layer : 16 * layer + count]
+        out[:, 128:144] = tail[0:count, 16 * layer : 16 * layer + 16]
+    for tap in range(9):
+        block = tail[:, 0:16] if tap == 8 else rows[0:16, 16 * tap : 16 * tap + 16]
+        first_out[:, 11 * tap : 11 * tap + CL] = block[:, 0:CL]
+        first_out[:, 11 * tap + CL : 11 * tap + CL + 1] = block[:, HCH : HCH + 1]
 
     def sent_forward(shift):
         if shift:
@@ -760,29 +794,36 @@
             edge_back(side, shift + 1).wait_send()
 
     for_lat(sent_forward)
-    for k in range(1, nlon):
-        scatter_copy(k).wait_send()
-        full_copy(k).wait_send()
-    for k in range(1, group):
-        part_copy(k).wait_send()
-
-    @pl.when(lat == top)
-    def _():
-        for side in range(2):
-            edge_back(side, 2, True).wait_send()
+    half_copy().wait_send()
+    total_copy().wait_send()
+    for k in range(1, plane):
+        plane_copy(k).wait_send()
+    for k in range(1, nz):
+        column_copy(k).wait_send()
+
+    @pl.when(lat == top)
+    def _():
         for k in range(1, nlon):
             for copy in fold_copies(k) + unfold_copies(k):
                 copy.wait_send()
 
 
+def hand_over(*refs):
+    sources, targets, sem = refs[:6], refs[6:12], refs[12]
+    copies = [pltpu.make_async_copy(src, dst, sem.at[k]) for k, (src, dst) in enumerate(zip(sources, targets))]
+    for copy in copies:
+        copy.start()
+    for copy in copies:
+        copy.wait()
+
+
 def solution(mesh):
     nlon, nlat, nens = (mesh.shape[axis] for axis in ("lon", "lat", "ens"))
-    group = nlat * nens
+    plane = nlat * nens
 
     def local(temp, height, flow, land_sea, fold, w_first, w_second, w_third, temp_bar, height_bar, flow_bar):
         vmem = pltpu.VMEM
         dma = pltpu.SemaphoreType.DMA
-        chunk = 64 // nlon
         scratch = [
             vmem((2, 4, 48, LANES), F32),
             vmem((2, LEV, 32, LANES), F32),
@@ -814,15 +855,17 @@
             vmem((2, 3, 48, LANES), F32),
             vmem((2, LEV, 32, LANES), F32),
             vmem((3, 2, 16, LANES), F32),
-            vmem((2, 4, 2, 16, LANES), F32),
+            vmem((2, 3, 2, 16, LANES), F32),
             vmem((2, 3, 16, LANES), F32),
             vmem((2, LEV, 8, LANES), F32),
-            vmem((nlon, 40, LANES), F32),
-            vmem((nlon, 40, LANES), F32),
-            vmem((nlon, chunk, LANES), F32),
-            vmem((nlon, chunk, LANES), F32),
-            vmem((group, chunk, LANES), F32),
-            vmem((nlon, chunk, LANES), F32),
+            vmem((nlon, 48, LANES), F32),
+            vmem((nlon, 48, LANES), F32),
+            vmem((2, 40, LANES), F32),
+            vmem((2, 24, LANES), F32),
+            vmem((24, LANES), F32),
+            vmem((plane, 24, LANES), F32),
+            vmem((nlon // 2, 24, LANES), F32),
+            vmem((2, 24, LANES), F32),
             dma((11,)),
             dma((4,)),
             dma((4,)),
@@ -836,8 +879,12 @@
             dma((2, 4)),
             dma((2, nlon)),
             dma((2, nlon)),
-            dma((3, max(nlon, group))),
-            dma((3, max(nlon, group))),
+            dma((2,)),
+            dma((2,)),
+            dma((plane,)),
+            dma((plane,)),
+            dma((nlon // 2,)),
+            dma((nlon // 2,)),
         ]
         out_shape = (
             jax.ShapeDtypeStruct(temp.shape, F32),
@@ -847,23 +894,30 @@
             jax.ShapeDtypeStruct(w_second.shape, F32),
             jax.ShapeDtypeStruct(w_third.shape, F32),
         )
-        return pl.pallas_call(
+        results = pl.pallas_call(
             functools.partial(kernel, (nlon, nlat, nens)),
             out_shape=out_shape,
-            in_specs=[pl.BlockSpec(memory_space=pl.ANY)] * 11,
+            in_specs=[pl.BlockSpec(memory_space=pltpu.HBM)] * 11,
             out_specs=[pl.BlockSpec(memory_space=pltpu.VMEM)] * 6,
             scratch_shapes=scratch,
             compiler_params=pltpu.CompilerParams(
-                collective_id=0, has_side_effects=True, vmem_limit_bytes=32 * 1024 * 1024
+                collective_id=0, has_side_effects=True, vmem_limit_bytes=60 * 1024 * 1024
             ),
         )(temp, height, flow, land_sea, fold, w_first, w_second, w_third, temp_bar, height_bar, flow_bar)
+        return pl.pallas_call(
+            hand_over,
+            out_shape=out_shape,
+            in_specs=[pl.BlockSpec(memory_space=pltpu.VMEM)] * 6,
+            out_specs=[pl.BlockSpec(memory_space=pltpu.HBM)] * 6,
+            scratch_shapes=[dma((6,))],
+        )(*results)
 
     field = P("ens", None, "lat", "lon")
-    plane = P("ens", "lat", "lon")
+    surface = P("ens", "lat", "lon")
     return jax.shard_map(
         local,
         mesh=mesh,
-        in_specs=(field, plane, field, P("lat", "lon"), P(), P(), P(), P(), field, plane, field),
-        out_specs=(field, plane, field, P(), P(), P()),
+        in_specs=(field, surface, field, P("lat", "lon"), P(), P(), P(), P(), field, surface, field),
+        out_specs=(field, surface, field, P(), P(), P()),
         check_vma=False,
     )

time: 57.2 us -> 45.8 us (0.80)
  the two profiles are of different devices: /device:TPU:29 before, /device:TPU:1 now
where the time goes in v2:
time: 45.8 us; the launch traced here: 45.7 us
  Pallas kernels  45 us (98%)
  between operations  0.64 us (1%)
    pallas_call x1, Pallas kernels, local(): pl.pallas_call(functools.partial(kernel, (nlon, nlat, nens)), out_shape=o...  43.4 us
    pallas_call x1, Pallas kernels, local(): pl.pallas_call(hand_over, out_shape=out_shape, in_specs=[pl.BlockSpec(mem...  1.64 us

profile of v2, /device:TPU:1, one launch (start us, length us, event | category | flops | bytes accessed | tf_op | source)
XLA Modules:
  0.0 45.7 jit_solution(13627663782971532925)
XLA Ops:
  0.6 43.4 %shard_map.154 = (f32[1,12,16,128]{3,2,1,0:T(8,128)}, f32[1,16,128]{2,1,0:T(8,128)}, f32[1,2,16,128]{3,2,1,0:T(8,128)}, f32[16,99]{1,0:T(8,128)}, f32[16,144]{1,0:T(8,128)}, /*index=5*/f32[10,144]{1,0:T(8,128)}) custom-call(f32[1,12,16,128]{3,2,1,0:T(8,128)} %temp.1, f32[1,16,128]{2,1,0:T(8,128)} %height.1, f32[1,2,16,128]{3,2,1,0:T(8,128)} %flow.1, ...), custom_call_target="tpu_custom_call" | custom-call | tf_op jit(solution)/shard_map/pallas_call | solution.py:897
  44.0 1.6 %shard_map.155 = (f32[1,12,16,128]{3,2,1,0:T(8,128)}, f32[1,16,128]{2,1,0:T(8,128)}, f32[1,2,16,128]{3,2,1,0:T(8,128)}, f32[16,99]{1,0:T(8,128)}, f32[16,144]{1,0:T(8,128)}, /*index=5*/f32[10,144]{1,0:T(8,128)}) custom-call(f32[1,12,16,128]{3,2,1,0:T(8,128)} %get-tuple-element.12.refs_0_, f32[1,16,128]{2,1,0:T(8,128)} %get-tuple-element.13.refs_1_, ...), custom_call_target="tpu_custom_call" | custom-call | tf_op jit(solution)/shard_map/pallas_call | solution.py:907

commit v3 on v2

--- a/solution.py
+++ b/solution.py
@@ -15,7 +15,7 @@
 SUB = 4
 LEV = 12
 CL = 10
-RIM = 11
+RIM = 10
 TRIM = 3
 HCH = 12
 LANES = 128
@@ -180,6 +180,8 @@
     msg_in,
     fold_surf,
     fold_trac,
+    select_in,
+    select_out,
     g3_rows,
     xs1,
     xs2,
@@ -238,41 +240,6 @@
             src_ref=src, dst_ref=dst, send_sem=send, recv_sem=recv, device_id=device, device_id_type=MESH
         )
 
-    barrier = pltpu.get_barrier_semaphore()
-
-    def greet(**device):
-        pl.semaphore_signal(barrier, inc=1, device_id=device, device_id_type=MESH)
-
-    def plane_device(index):
-        return dict(lon=lax.rem(index // ny, 2) * nz + z, lat=lax.rem(index, ny) * 2 + core, ens=index // (2 * ny))
-
-    def column_device(index):
-        return dict(lon=(lon // nz) * nz + index)
-
-    for k in range(1, plane):
-        greet(**plane_device(lax.rem(place + k, plane)))
-    for k in range(1, nz):
-        greet(**column_device(lax.rem(z + k, nz)))
-    greet(lon=left)
-    greet(lon=right)
-
-    @pl.when(lat > 0)
-    def _():
-        greet(lat=lat - 1)
-        greet(lon=left, lat=lat - 1)
-        greet(lon=right, lat=lat - 1)
-
-    @pl.when(lat < top)
-    def _():
-        greet(lat=lat + 1)
-        greet(lon=left, lat=lat + 1)
-        greet(lon=right, lat=lat + 1)
-
-    @pl.when(lat == top)
-    def _():
-        for k in range(1, nlon):
-            greet(lon=lax.rem(lon + k, nlon))
-
     loads = [
         (temp.at[0], trac.at[0, :, 8:24, :]),
         (height.at[0], surf.at[0, 0, 16:32, :]),
@@ -290,17 +257,70 @@
     for load in loads:
         load.start()
 
+    barrier = pltpu.get_barrier_semaphore()
+
+    def greet(**device):
+        pl.semaphore_signal(barrier, inc=1, device_id=device, device_id_type=MESH)
+
+    def bits(value, size):
+        return [lax.rem(value // 2**k, 2) for k in range(size.bit_length() - 1)]
+
+    def flip(value, digits, mask):
+        return value + sum((1 - 2 * digit) * 2**k for k, digit in enumerate(digits) if mask >> k & 1)
+
+    def reach(mask):
+        return (0, 1, 2, 3, 4, 3, 2, 3)[mask] if mask < 8 else 1 + reach(mask - 8)
+
+    def plane_reach(mask):
+        return sum((0, 1, 2, 1)[part] for part in (mask // ny, mask % ny))
+
+    x, y = ens * 2 + lon // nz, lat // 2
+    x_bits, y_bits, lon_bits = bits(x, 2 * nens), bits(y, ny), bits(lon, nlon)
+    plane_masks = sorted(range(1, plane), key=plane_reach, reverse=True)
+    column_masks = sorted(range(1, nz), key=reach, reverse=True)
+    lon_masks = sorted(range(1, nlon), key=reach, reverse=True)
+
+    def plane_peer(mask):
+        px, py = flip(x, x_bits, mask // ny), flip(y, y_bits, mask % ny)
+        device = dict(lon=lax.rem(px, 2) * nz + z, lat=py * 2 + core, ens=px // 2)
+        return px * ny + py, device
+
+    def lon_peer(mask):
+        return flip(lon, lon_bits, mask)
+
+    for mask in plane_masks:
+        greet(**plane_peer(mask)[1])
+    for mask in column_masks:
+        greet(lon=lon_peer(mask))
+    greet(lon=left)
+    greet(lon=right)
+
+    @pl.when(lat > 0)
+    def _():
+        greet(lat=lat - 1)
+        greet(lon=left, lat=lat - 1)
+        greet(lon=right, lat=lat - 1)
+
+    @pl.when(lat < top)
+    def _():
+        greet(lat=lat + 1)
+        greet(lon=left, lat=lat + 1)
+        greet(lon=right, lat=lat + 1)
+
+    @pl.when(lat == top)
+    def _():
+        for mask in lon_masks:
+            greet(lon=lon_peer(mask))
+
     inputs[:, 32 * (HCH + 1) :, :] = jnp.zeros((2, 32 * (15 - HCH), LANES), F32)
     for ref, rows in ((gs3, 20), (gs2, 22), (gs1, 24)):
         for tile in range(2):
             for row in (0, 1, rows - 2, rows - 1):
                 ref[tile, row] = jnp.zeros((48, LANES), BF16)
     back[...] = jnp.zeros_like(back)
-    fold_surf[lon, 40:48, :] = jnp.zeros((8, LANES), F32)
-    fold_trac[lon, 32:40, :] = jnp.zeros((8, LANES), F32)
     for ref in (unfold_surf, unfold_trac):
-        ref[lon, 32:40, :] = jnp.zeros((8, LANES), F32)
-    unfold_edge[:, 32:40, :] = jnp.zeros((2, 8, LANES), F32)
+        ref[lon, 24:32, :] = jnp.zeros((8, LANES), F32)
+    unfold_edge[:, 24:32, :] = jnp.zeros((2, 8, LANES), F32)
 
     @pl.when(lat == 0)
     def _():
@@ -346,30 +366,20 @@
             msg_out, msg_in.at[side, 1 - shift], m_send.at[slot], m_recv.at[slot], lon=(right, left)[side], lat=lat + shift
         )
 
-    def fold_copies(k):
-        peer = lax.rem(lon + k, nlon)
-        return (
-            remote(fold_surf.at[lon], fold_surf.at[lon], fold_send.at[0, k], fold_recv.at[0, k], lon=peer),
-            remote(fold_trac.at[lon], fold_trac.at[lon], fold_send.at[1, k], fold_recv.at[1, k], lon=peer),
-        )
-
-    def fold_arrivals(k):
-        source = lax.rem(lon + nlon - k, nlon)
-        return (
-            remote(fold_surf.at[lon], fold_surf.at[source], fold_send.at[0, k], fold_recv.at[0, k], lon=source),
-            remote(fold_trac.at[lon], fold_trac.at[source], fold_send.at[1, k], fold_recv.at[1, k], lon=source),
-        )
-
-    @pl.when(lat == top)
-    def _():
-        for f in range(4):
-            for m in range(RIM):
-                row = RIM * f + m
-                fold_surf[lon, row : row + 1, :] = surf[0, f, 31 - m : 32 - m, :]
-        for c in range(LEV):
-            for m in range(TRIM):
-                row = TRIM * c + m
-                fold_trac[lon, row : row + 1, :] = trac[0, c, 23 - m : 24 - m, :]
+    def lon_copy(ref, mask, send, recv, arrival=False):
+        peer = lon_peer(mask)
+        return remote(ref.at[lon], ref.at[peer if arrival else lon], send.at[mask], recv.at[mask], lon=peer)
+
+    def ghost_rows(width, count):
+        full = [(f, m) for f in range(min(count, CL)) for m in range(width)]
+        return full + [(f, 0) for f in range(CL, count)]
+
+    @pl.when(lat == top)
+    def _():
+        for row, (f, m) in enumerate(ghost_rows(RIM, 4)):
+            fold_surf[lon, row : row + 1, :] = surf[0, f, 31 - m : 32 - m, :]
+        for row, (c, m) in enumerate(ghost_rows(TRIM, LEV)):
+            fold_trac[lon, row : row + 1, :] = trac[0, c, 23 - m : 24 - m, :]
 
     pl.semaphore_wait(
         barrier,
@@ -388,8 +398,8 @@
 
     @pl.when(lat == top)
     def _():
-        for k in range(1, nlon):
-            fold_copies(k)[0].start()
+        for mask in lon_masks:
+            lon_copy(fold_surf, mask, fold_send.at[0], fold_recv.at[0]).start()
 
     def start_forward(shift):
         if shift:
@@ -402,8 +412,8 @@
 
     @pl.when(lat == top)
     def _():
-        for k in range(1, nlon):
-            fold_copies(k)[1].start()
+        for mask in lon_masks:
+            lon_copy(fold_trac, mask, fold_send.at[1], fold_recv.at[1]).start()
 
     for k in range(4, 11):
         loads[k].wait()
@@ -433,18 +443,28 @@
         store_shifted(gs3, row + 2, (own, jnp.zeros_like(own)))
 
     shift_s = fold_s[0] + 1
-    base = shift_s - 139 - LANES * lon + LANES * (2 * nlon)
+    base = shift_s - (LANES + RIM) - LANES * lon + LANES * (2 * nlon)
     tile0 = base // LANES
     offset = shift_s - 1 - LANES * lon + LANES * (2 * nlon) - LANES * tile0
 
     def mirrored(ref):
         return jnp.concatenate([ref[lax.rem(tile0 + j, nlon)] for j in range(3)], axis=1)
 
-    def mirror_matrix():
+    @pl.when(lat == top)
+    def _():
         source = lax.broadcasted_iota(jnp.int32, (3 * LANES, 2 * LANES), 0)
         column = lax.broadcasted_iota(jnp.int32, (3 * LANES, 2 * LANES), 1)
         column = jnp.where(column < LANES + LANES // 2, column, column - 2 * LANES)
-        return jnp.where(source + column == offset, 1.0, 0.0).astype(BF16)
+        select_in[...] = jnp.where(source + column == offset, 1.0, 0.0).astype(BF16)
+        lane = lax.broadcasted_iota(jnp.int32, (LANES, LANES), 0)
+        column = lax.broadcasted_iota(jnp.int32, (LANES, LANES), 1)
+        halo = jnp.where(lane < LANES // 2, lane + LANES, lane - LANES)
+        for k, at in enumerate((lane, halo)):
+            for j in range(3):
+                first = LANES * (3 * k + j)
+                select_out[first : first + LANES, :] = jnp.where(at + LANES * j + column == offset, 1.0, 0.0).astype(
+                    BF16
+                )
 
     left_s = slot_mask(16, RIM, 4, 0)
     left_t = slot_mask(16, TRIM, LEV, 0)
@@ -469,10 +489,10 @@
 
     @pl.when(lat == top)
     def _():
-        select = mirror_matrix()
-        for k in range(1, nlon):
-            fold_arrivals(k)[0].wait_recv()
-        ghost = permute_columns(mirrored(fold_surf), select)
+        for mask in lon_masks:
+            lon_copy(fold_surf, mask, fold_send.at[0], fold_recv.at[0], True).wait_recv()
+        window = jnp.concatenate([mirrored(fold_surf), jnp.zeros((8, 3 * LANES), F32)], axis=0)
+        ghost = permute_columns(window, select_in[...])
         for f in range(4):
             rows = ghost[RIM * f : RIM * f + RIM]
             rows = -rows if f in (1, 2) else rows
@@ -486,15 +506,13 @@
 
     @pl.when(lat == top)
     def _():
-        select = mirror_matrix()
-        for k in range(1, nlon):
-            fold_arrivals(k)[1].wait_recv()
-        ghost = permute_columns(mirrored(fold_trac), select)
+        for mask in lon_masks:
+            lon_copy(fold_trac, mask, fold_send.at[1], fold_recv.at[1], True).wait_recv()
+        ghost = permute_columns(mirrored(fold_trac), select_in[...])
         for c in range(LEV):
-            rows = ghost[TRIM * c : TRIM * c + TRIM]
+            first, count = (TRIM * c, TRIM) if c < CL else (TRIM * CL + c - CL, 1)
             for tile in range(2):
-                trac[tile, c, 24 : 24 + TRIM, :] = rows[:, LANES * tile : LANES * tile + LANES]
-
+                trac[tile, c, 24 : 24 + count, :] = ghost[first : first + count, LANES * tile : LANES * tile + LANES]
 
     for tile in range(2):
         for c in range(LEV):
@@ -541,19 +559,15 @@
     def half_copy():
         return remote(halves.at[1 - core], half_in, pair_send.at[0], pair_recv.at[0], lat=lat + 1 - 2 * core)
 
-    def plane_copy(k, arrival=False):
-        other = lax.rem(place + (plane - k if arrival else k), plane)
+    def plane_copy(mask, arrival=False):
+        other, device = plane_peer(mask)
         slot = other if arrival else place
-        return remote(
-            plane_in.at[place], plane_in.at[slot], plane_send.at[k], plane_recv.at[k], **plane_device(other)
-        )
-
-    def column_copy(k, arrival=False):
-        other = lax.rem(z + (nz - k if arrival else k), nz)
-        slot = other if arrival else z
-        return remote(
-            column_in.at[z], column_in.at[slot], column_send.at[k], column_recv.at[k], **column_device(other)
-        )
+        return remote(plane_in.at[place], plane_in.at[slot], plane_send.at[mask], plane_recv.at[mask], **device)
+
+    def column_copy(mask, arrival=False):
+        peer = lon_peer(mask)
+        slot = lax.rem(peer, nz) if arrival else z
+        return remote(column_in.at[z], column_in.at[slot], column_send.at[mask], column_recv.at[mask], lon=peer)
 
     def total_copy(arrival=False):
         slot = 1 - core if arrival else core
@@ -613,41 +627,25 @@
             remote(tg.at[0, :, rows_t, :], back_trac.at[slot], b_send.at[1, slot], b_recv.at[1, slot], lat=lat + to),
         )
 
-    def unfold_copies(k):
-        peer = lax.rem(lon + k, nlon)
-        return (
-            remote(unfold_surf.at[lon], unfold_surf.at[lon], unfold_send.at[0, k], unfold_recv.at[0, k], lon=peer),
-            remote(unfold_trac.at[lon], unfold_trac.at[lon], unfold_send.at[1, k], unfold_recv.at[1, k], lon=peer),
-        )
-
-    def unfold_arrivals(k):
-        source = lax.rem(lon + nlon - k, nlon)
-        return (
-            remote(unfold_surf.at[lon], unfold_surf.at[source], unfold_send.at[0, k], unfold_recv.at[0, k], lon=source),
-            remote(unfold_trac.at[lon], unfold_trac.at[source], unfold_send.at[1, k], unfold_recv.at[1, k], lon=source),
-        )
-
     def pack_ghosts(grads, first, count, width, out, edge):
-        for f in range(count):
-            for j in range(width):
-                row, ghost = width * f + j, first + width - 1 - j
-                out[lon, row : row + 1, :] = grads[0, f, ghost : ghost + 1, :]
-                edge[row : row + 1, :] = grads[1, f, ghost : ghost + 1, :]
-        out[lon, 40:48, :] = pack_edges([edge[8 * g : 8 * g + 8, :] for g in range(5)], width)
+        for row, (f, m) in enumerate(ghost_rows(width, count)):
+            out[lon, row : row + 1, :] = grads[0, f, first + m : first + m + 1, :]
+            edge[row : row + 1, :] = grads[1, f, first + m : first + m + 1, :]
+        out[lon, 32:40, :] = pack_edges([edge[8 * g : 8 * g + 8, :] for g in range(4)], width)
 
     @pl.when(lat == top)
     def _():
         pack_ghosts(tg, 24, LEV, TRIM, unfold_trac, unfold_edge.at[0])
-        for k in range(1, nlon):
-            unfold_copies(k)[1].start()
+        for mask in lon_masks:
+            lon_copy(unfold_trac, mask, unfold_send.at[1], unfold_recv.at[1]).start()
 
     pl.when(lat > 0)(lambda: lat_back(False)[1].start())
     pl.when(lat < top)(lambda: lat_back(True)[1].start())
 
     half_copy().wait_recv()
     plane_in[place] = halves[core] + half_in[...]
-    for k in range(1, plane):
-        plane_copy(k).start()
+    for mask in plane_masks:
+        plane_copy(mask).start()
 
     def own_rows(x):
         zero16 = jnp.zeros((16, LANES), F32)
@@ -687,8 +685,8 @@
     @pl.when(lat == top)
     def _():
         pack_ghosts(sg, 32, 3, RIM, unfold_surf, unfold_edge.at[1])
-        for k in range(1, nlon):
-            unfold_copies(k)[0].start()
+        for mask in lon_masks:
+            lon_copy(unfold_surf, mask, unfold_send.at[0], unfold_recv.at[0]).start()
 
     def start_back(shift):
         if shift:
@@ -701,11 +699,30 @@
     right_s = slot_mask(16, RIM, 3, RIM)
     right_t = slot_mask(16, TRIM, LEV, TRIM)
 
-    for k in range(1, plane):
-        plane_copy(k, True).wait_recv()
+    def sent_forward(shift):
+        if shift:
+            for copy in lat_copies(shift > 0):
+                copy.wait_send()
+        for side in range(2):
+            edge_copy(side, shift).wait_send()
+
+    for_lat(sent_forward)
+
+    @pl.when(lat == top)
+    def _():
+        for mask in lon_masks:
+            for part, ref in enumerate((fold_surf, fold_trac)):
+                lon_copy(ref, mask, fold_send.at[part], fold_recv.at[part]).wait_send()
+
+    half_copy().wait_send()
+    for mask in plane_masks:
+        plane_copy(mask).wait_send()
+
+    for mask in plane_masks:
+        plane_copy(mask, True).wait_recv()
     column_in[z] = sum_slots(plane_in, plane)
-    for k in range(1, nz):
-        column_copy(k).start()
+    for mask in column_masks:
+        column_copy(mask).start()
 
     def wait_back(shift):
         if shift:
@@ -730,42 +747,42 @@
         ghosts = jnp.concatenate([back_trac[0, c], back_trac[1, c]], axis=0)
         temp_out[0, c] = tg[0, c, 8:24, :] + ghosts + unpack_edge(packed, TRIM, c)
 
-    for k in range(1, nz):
-        column_copy(k, True).wait_recv()
+    def sent_back(shift):
+        if shift:
+            for copy in lat_back(shift > 0):
+                copy.wait_send()
+        for side in range(2):
+            edge_back(side, shift + 1).wait_send()
+
+    for_lat(sent_back)
+
+    for mask in column_masks:
+        column_copy(mask, True).wait_recv()
     totals[core] = sum_slots(column_in, nz)
     total_copy().start()
 
     @pl.when(lat == top)
     def _():
-        lane = lax.broadcasted_iota(jnp.int32, (LANES, LANES), 0)
-        column = lax.broadcasted_iota(jnp.int32, (LANES, LANES), 1)
-        halo = jnp.where(lane < LANES // 2, lane + LANES, lane - LANES)
-        select = jnp.concatenate(
-            [jnp.where(at + LANES * j + column == offset, 1.0, 0.0) for at in (lane, halo) for j in range(3)], axis=0
-        ).astype(BF16)
-
         def unfold(ref, width):
             tiles = [ref[lax.rem(tile0 + j, nlon)] for j in range(3)]
             edges = [
-                jnp.concatenate([unpack_edge(tile[40:48], width, g) for g in range(5)], axis=0) for tile in tiles
+                jnp.concatenate([unpack_edge(tile[32:40], width, g) for g in range(4)], axis=0) for tile in tiles
             ]
-            return permute_columns(jnp.concatenate([tile[0:40] for tile in tiles] + edges, axis=1), select)
-
-        for k in range(1, nlon):
-            unfold_arrivals(k)[1].wait_recv()
+            return permute_columns(jnp.concatenate([tile[0:32] for tile in tiles] + edges, axis=1), select_out[...])
+
+        for mask in lon_masks:
+            lon_copy(unfold_trac, mask, unfold_send.at[1], unfold_recv.at[1], True).wait_recv()
         ghost = unfold(unfold_trac, TRIM)
-        for c in range(LEV):
-            temp_out[0, c, 16 - TRIM : 16, :] = (
-                temp_out[0, c, 16 - TRIM : 16, :] + ghost[TRIM * c : TRIM * c + TRIM]
-            )
-        for k in range(1, nlon):
-            unfold_arrivals(k)[0].wait_recv()
+        for row, (c, m) in enumerate(ghost_rows(TRIM, LEV)):
+            temp_out[0, c, 15 - m : 16 - m, :] = temp_out[0, c, 15 - m : 16 - m, :] + ghost[row : row + 1]
+        for mask in lon_masks:
+            lon_copy(unfold_surf, mask, unfold_send.at[0], unfold_recv.at[0], True).wait_recv()
         ghost = unfold(unfold_surf, RIM)
-        height_out[0, 16 - RIM : 16, :] = height_out[0, 16 - RIM : 16, :] + ghost[0:RIM]
-        for f in (1, 2):
-            flow_out[0, f - 1, 16 - RIM : 16, :] = (
-                flow_out[0, f - 1, 16 - RIM : 16, :] - ghost[RIM * f : RIM * f + RIM]
-            )
+        for row, (f, m) in enumerate(ghost_rows(RIM, 3)):
+            if f == 0:
+                height_out[0, 15 - m : 16 - m, :] = height_out[0, 15 - m : 16 - m, :] + ghost[row : row + 1]
+            else:
+                flow_out[0, f - 1, 15 - m : 16 - m, :] = flow_out[0, f - 1, 15 - m : 16 - m, :] - ghost[row : row + 1]
 
     total_copy(True).wait_recv()
     scale = 1.0 / math.sqrt(nens * nlat * 16 * nlon * LANES)
@@ -783,29 +800,15 @@
         first_out[:, 11 * tap : 11 * tap + CL] = block[:, 0:CL]
         first_out[:, 11 * tap + CL : 11 * tap + CL + 1] = block[:, HCH : HCH + 1]
 
-    def sent_forward(shift):
-        if shift:
-            for copy in lat_copies(shift > 0):
-                copy.wait_send()
-            for copy in lat_back(shift > 0):
-                copy.wait_send()
-        for side in range(2):
-            edge_copy(side, shift).wait_send()
-            edge_back(side, shift + 1).wait_send()
-
-    for_lat(sent_forward)
-    half_copy().wait_send()
+    for mask in column_masks:
+        column_copy(mask).wait_send()
     total_copy().wait_send()
-    for k in range(1, plane):
-        plane_copy(k).wait_send()
-    for k in range(1, nz):
-        column_copy(k).wait_send()
-
-    @pl.when(lat == top)
-    def _():
-        for k in range(1, nlon):
-            for copy in fold_copies(k) + unfold_copies(k):
-                copy.wait_send()
+
+    @pl.when(lat == top)
+    def _():
+        for mask in lon_masks:
+            for part, ref in enumerate((unfold_surf, unfold_trac)):
+                lon_copy(ref, mask, unfold_send.at[part], unfold_recv.at[part]).wait_send()
 
 
 def hand_over(*refs):
@@ -840,8 +843,10 @@
             vmem((3, 16, 144), F32),
             vmem((2, 16, LANES), F32),
             vmem((2, 3, 2, 16, LANES), F32),
-            vmem((nlon, 48, LANES), F32),
             vmem((nlon, 40, LANES), F32),
+            vmem((nlon, 32, LANES), F32),
+            vmem((3 * LANES, 2 * LANES), BF16),
+            vmem((6 * LANES, LANES), BF16),
             vmem((16 * 16, LANES), F32),
             vmem((2, 22, 48, LANES), BF16),
             vmem((2, 20, 48, LANES), BF16),
@@ -858,9 +863,9 @@
             vmem((2, 3, 2, 16, LANES), F32),
             vmem((2, 3, 16, LANES), F32),
             vmem((2, LEV, 8, LANES), F32),
-            vmem((nlon, 48, LANES), F32),
-            vmem((nlon, 48, LANES), F32),
-            vmem((2, 40, LANES), F32),
+            vmem((nlon, 40, LANES), F32),
+            vmem((nlon, 40, LANES), F32),
+            vmem((2, 32, LANES), F32),
             vmem((2, 24, LANES), F32),
             vmem((24, LANES), F32),
             vmem((plane, 24, LANES), F32),
@@ -896,7 +901,7 @@
         )
         results = pl.pallas_call(
             functools.partial(kernel, (nlon, nlat, nens)),
-            out_shape=out_shape,
+            out_shape=tuple(pltpu.VMEM(o.shape, F32) for o in out_shape),
             in_specs=[pl.BlockSpec(memory_space=pltpu.HBM)] * 11,
             out_specs=[pl.BlockSpec(memory_space=pltpu.VMEM)] * 6,
             scratch_shapes=scratch,
@@ -907,9 +912,10 @@
         return pl.pallas_call(
             hand_over,
             out_shape=out_shape,
-            in_specs=[pl.BlockSpec(memory_space=pltpu.VMEM)] * 6,
+            in_specs=[pl.BlockSpec(memory_space=pl.ANY)] * 6,
             out_specs=[pl.BlockSpec(memory_space=pltpu.HBM)] * 6,
             scratch_shapes=[dma((6,))],
+            compiler_params=pltpu.CompilerParams(vmem_limit_bytes=1024 * 1024),
         )(*results)
 
     field = P("ens", None, "lat", "lon")

time: 45.8 us -> 41.2 us (0.90)
  Pallas kernels: 45 us -> 40.4 us
    pallas_call x1, Pallas kernels: 43.4 us -> 39.7 us  [local(): pl.pallas_call(functools.partial(kernel, (nlon, nlat, nens)), out_shape=t...]
    pallas_call x1, Pallas kernels: 1.64 us -> 0.71 us  [local(): pl.pallas_call(hand_over, out_shape=out_shape, in_specs=[pl.BlockSpec(mem...]
where the time goes in v3:
time: 41.2 us; the launch traced here: 41.1 us
  Pallas kernels  40.4 us (98%)
  between operations  0.64 us (2%)
    pallas_call x1, Pallas kernels, local(): pl.pallas_call(functools.partial(kernel, (nlon, nlat, nens)), out_shape=t...  39.7 us

profile of v3, /device:TPU:1, one launch (start us, length us, event | category | flops | bytes accessed | tf_op | source)
XLA Modules:
  0.0 41.1 jit_solution(16697988159839598874)
XLA Ops:
  0.6 39.7 %shard_map.154 = (f32[1,12,16,128]{3,2,1,0:T(8,128)S(1)}, f32[1,16,128]{2,1,0:T(8,128)S(1)}, f32[1,2,16,128]{3,2,1,0:T(8,128)S(1)}, f32[16,99]{1,0:T(8,128)S(1)}...) custom-call(f32[1,12,16,128]{3,2,1,0:T(8,128)} %temp.1, f32[1,16,128]{2,1,0:T(8,128)} %height.1, f32[1,2,16,128]{3,2,1,0:T(8,128)} %flow.1, ...), custom_call_target="tpu_custom_call" | custom-call | tf_op jit(solution)/shard_map/pallas_call | solution.py:902
  40.3 0.7 %shard_map.155 = (f32[1,12,16,128]{3,2,1,0:T(8,128)}, f32[1,16,128]{2,1,0:T(8,128)}, f32[1,2,16,128]{3,2,1,0:T(8,128)}, f32[16,99]{1,0:T(8,128)}, f32[16,144]{1,0:T(8,128)}, /*index=5*/f32[10,144]{1,0:T(8,128)}) custom-call(f32[1,12,16,128]{3,2,1,0:T(8,128)S(1)} %get-tuple-element.12.refs_0_, f32[1,16,128]{2,1,0:T(8,128)S(1)} %get-tuple-element.13.refs_1_, ...), custom_call_target="tpu_custom_call" | custom-call | tf_op jit(solution)/shard_map/pallas_call | solution.py:912

commit v4 on v3

--- a/solution.py
+++ b/solution.py
@@ -396,11 +396,6 @@
         fn(0)
         pl.when(lat < top)(functools.partial(fn, 1))
 
-    @pl.when(lat == top)
-    def _():
-        for mask in lon_masks:
-            lon_copy(fold_surf, mask, fold_send.at[0], fold_recv.at[0]).start()
-
     def start_forward(shift):
         if shift:
             for copy in lat_copies(shift > 0):
@@ -409,6 +404,11 @@
             edge_copy(side, shift).start()
 
     for_lat(start_forward)
+
+    @pl.when(lat == top)
+    def _():
+        for mask in lon_masks:
+            lon_copy(fold_surf, mask, fold_send.at[0], fold_recv.at[0]).start()
 
     @pl.when(lat == top)
     def _():
@@ -504,6 +504,46 @@
         h, e, n = step_forward(h, e, n, wet)
     new_e, new_n = e[0][16:32], n[0][16:32]
 
+    for tile in range(2):
+        for c in range(LEV):
+            inputs[tile, 32 * c : 32 * c + 32, :] = trac[tile, c]
+        inputs[tile, 32 * HCH : 32 * HCH + 32, :] = h[tile][8:40]
+
+    def activate(weight, xs, act_ref, out, rows):
+        for row in rows:
+            act = lift(jnp.tanh)(conv_row(weight, xs, row))
+            for tile in range(2):
+                act_ref[tile, row] = act[tile]
+            store_shifted(out, row, act)
+
+    def weight_sum(total, gs, xs, rows):
+        for row in rows:
+            grad = jnp.concatenate([gs[tile, row + 2, 16:32, :] for tile in range(2)], axis=1)
+            total = total + contract(grad, patch(xs, row))
+        return total
+
+    def back_layer(weight, gs, act_ref, out, rows):
+        for row in rows:
+            grad = conv_row(weight, gs, row)
+            act = tuple(act_ref[tile, row] for tile in range(2))
+            store_shifted(out, row + 2, lift(lambda g, a: g * (1.0 - a * a))(grad, act))
+
+    def closure(ends, sums):
+        rows = [range(*pair) for pair in ends]
+        for row in rows[0]:
+            store_shifted(xs1, row, tuple(inputs[tile, pl.ds(5 + row, 16, stride=32), :] for tile in range(2)))
+        activate(weight1, xs1, act1, xs2, rows[1])
+        activate(weight2, xs2, act2, xs3, rows[2])
+        back_layer(flip3, gs3, act2, gs2, rows[2])
+        sum3 = weight_sum(sums[2], gs3, xs3, rows[3])
+        back_layer(flip2, gs2, act1, gs1, rows[4])
+        sum2 = weight_sum(sums[1], gs2, xs2, rows[2])
+        sum1 = weight_sum(sums[0], gs1, xs1, rows[4])
+        return sum1, sum2, sum3
+
+    split = (19, 17, 15, 13, 15)
+    sums = closure([(0, at) for at in split], (jnp.zeros((16, 144), F32),) * 3)
+
     @pl.when(lat == top)
     def _():
         for mask in lon_masks:
@@ -512,43 +552,11 @@
         for c in range(LEV):
             first, count = (TRIM * c, TRIM) if c < CL else (TRIM * CL + c - CL, 1)
             for tile in range(2):
-                trac[tile, c, 24 : 24 + count, :] = ghost[first : first + count, LANES * tile : LANES * tile + LANES]
-
-    for tile in range(2):
-        for c in range(LEV):
-            inputs[tile, 32 * c : 32 * c + 32, :] = trac[tile, c]
-        inputs[tile, 32 * HCH : 32 * HCH + 32, :] = h[tile][8:40]
-    for row in range(22):
-        store_shifted(xs1, row, tuple(inputs[tile, pl.ds(5 + row, 16, stride=32), :] for tile in range(2)))
-    for row in range(20):
-        act = lift(jnp.tanh)(conv_row(weight1, xs1, row))
-        for tile in range(2):
-            act1[tile, row] = act[tile]
-        store_shifted(xs2, row, act)
-    for row in range(18):
-        act = lift(jnp.tanh)(conv_row(weight2, xs2, row))
-        for tile in range(2):
-            act2[tile, row] = act[tile]
-        store_shifted(xs3, row, act)
-
-    def weight_sum(gs, xs, rows):
-        total = jnp.zeros((16, 144), F32)
-        for row in range(rows):
-            grad = jnp.concatenate([gs[tile, row + 2, 16:32, :] for tile in range(2)], axis=1)
-            total = total + contract(grad, patch(xs, row))
-        return total
-
-    def back_layer(weight, gs, act_ref, out, rows):
-        for row in range(rows):
-            grad = conv_row(weight, gs, row)
-            act = tuple(act_ref[tile, row] for tile in range(2))
-            store_shifted(out, row + 2, lift(lambda g, a: g * (1.0 - a * a))(grad, act))
-
-    sum3 = weight_sum(gs3, xs3, 16)
-    back_layer(flip3, gs3, act2, gs2, 18)
-    sum2 = weight_sum(gs2, xs2, 18)
-    back_layer(flip2, gs2, act1, gs1, 20)
-    sum1 = weight_sum(gs1, xs1, 20)
+                rows = ghost[first : first + count, LANES * tile : LANES * tile + LANES]
+                trac[tile, c, 24 : 24 + count, :] = rows
+                inputs[tile, 32 * c + 24 : 32 * c + 24 + count, :] = rows
+
+    sum1, sum2, sum3 = closure(list(zip(split, (22, 20, 18, 16, 20))), sums)
 
     tail = jnp.concatenate([sum1[:, 128:144], sum2[:, 128:144], sum3[:, 128:144], jnp.zeros((16, 80), F32)], axis=1)
     tail = jnp.concatenate([tail[0:6, 0:48], tail[6:12, 0:48], tail[10:16, 0:32]], axis=1)
@@ -633,19 +641,17 @@
             edge[row : row + 1, :] = grads[1, f, first + m : first + m + 1, :]
         out[lon, 32:40, :] = pack_edges([edge[8 * g : 8 * g + 8, :] for g in range(4)], width)
 
+    half_copy().wait_recv()
+    column_in[z] = halves[core] + half_in[...]
+    for mask in column_masks:
+        column_copy(mask).start()
+
     @pl.when(lat == top)
     def _():
         pack_ghosts(tg, 24, LEV, TRIM, unfold_trac, unfold_edge.at[0])
-        for mask in lon_masks:
-            lon_copy(unfold_trac, mask, unfold_send.at[1], unfold_recv.at[1]).start()
 
     pl.when(lat > 0)(lambda: lat_back(False)[1].start())
     pl.when(lat < top)(lambda: lat_back(True)[1].start())
-
-    half_copy().wait_recv()
-    plane_in[place] = halves[core] + half_in[...]
-    for mask in plane_masks:
-        plane_copy(mask).start()
 
     def own_rows(x):
         zero16 = jnp.zeros((16, LANES), F32)
@@ -687,6 +693,8 @@
         pack_ghosts(sg, 32, 3, RIM, unfold_surf, unfold_edge.at[1])
         for mask in lon_masks:
             lon_copy(unfold_surf, mask, unfold_send.at[0], unfold_recv.at[0]).start()
+        for mask in lon_masks:
+            lon_copy(unfold_trac, mask, unfold_send.at[1], unfold_recv.at[1]).start()
 
     def start_back(shift):
         if shift:
@@ -715,14 +723,14 @@
                 lon_copy(ref, mask, fold_send.at[part], fold_recv.at[part]).wait_send()
 
     half_copy().wait_send()
+    for mask in column_masks:
+        column_copy(mask).wait_send()
+
+    for mask in column_masks:
+        column_copy(mask, True).wait_recv()
+    plane_in[place] = sum_slots(column_in, nz)
     for mask in plane_masks:
-        plane_copy(mask).wait_send()
-
-    for mask in plane_masks:
-        plane_copy(mask, True).wait_recv()
-    column_in[z] = sum_slots(plane_in, plane)
-    for mask in column_masks:
-        column_copy(mask).start()
+        plane_copy(mask).start()
 
     def wait_back(shift):
         if shift:
@@ -756,9 +764,9 @@
 
     for_lat(sent_back)
 
-    for mask in column_masks:
-        column_copy(mask, True).wait_recv()
-    totals[core] = sum_slots(column_in, nz)
+    for mask in plane_masks:
+        plane_copy(mask, True).wait_recv()
+    totals[core] = sum_slots(plane_in, plane)
     total_copy().start()
 
     @pl.when(lat == top)
@@ -800,8 +808,8 @@
         first_out[:, 11 * tap : 11 * tap + CL] = block[:, 0:CL]
         first_out[:, 11 * tap + CL : 11 * tap + CL + 1] = block[:, HCH : HCH + 1]
 
-    for mask in column_masks:
-        column_copy(mask).wait_send()
+    for mask in plane_masks:
+        plane_copy(mask).wait_send()
     total_copy().wait_send()
 
     @pl.when(lat == top)

time: 41.2 us -> 39.1 us (0.949)
  Pallas kernels: 40.4 us -> 38.3 us
    pallas_call x1, Pallas kernels: 39.7 us -> 37.6 us  [local(): pl.pallas_call(functools.partial(kernel, (nlon, nlat, nens)), out_shape=t...]
where the time goes in v4:
time: 39.1 us; the launch traced here: 39 us
  Pallas kernels  38.3 us (98%)
  between operations  0.64 us (2%)
    pallas_call x1, Pallas kernels, local(): pl.pallas_call(functools.partial(kernel, (nlon, nlat, nens)), out_shape=t...  37.6 us

profile of v4, /device:TPU:1, one launch (start us, length us, event | category | flops | bytes accessed | tf_op | source)
XLA Modules:
  0.0 39.0 jit_solution(17851984916680642755)
XLA Ops:
  0.6 37.6 %shard_map.154 = (f32[1,12,16,128]{3,2,1,0:T(8,128)S(1)}, f32[1,16,128]{2,1,0:T(8,128)S(1)}, f32[1,2,16,128]{3,2,1,0:T(8,128)S(1)}, f32[16,99]{1,0:T(8,128)S(1)}...) custom-call(f32[1,12,16,128]{3,2,1,0:T(8,128)} %temp.1, f32[1,16,128]{2,1,0:T(8,128)} %height.1, f32[1,2,16,128]{3,2,1,0:T(8,128)} %flow.1, ...), custom_call_target="tpu_custom_call" | custom-call | tf_op jit(solution)/shard_map/pallas_call | solution.py:910
  38.3 0.7 %shard_map.155 = (f32[1,12,16,128]{3,2,1,0:T(8,128)}, f32[1,16,128]{2,1,0:T(8,128)}, f32[1,2,16,128]{3,2,1,0:T(8,128)}, f32[16,99]{1,0:T(8,128)}, f32[16,144]{1,0:T(8,128)}, /*index=5*/f32[10,144]{1,0:T(8,128)}) custom-call(f32[1,12,16,128]{3,2,1,0:T(8,128)S(1)} %get-tuple-element.12.refs_0_, f32[1,16,128]{2,1,0:T(8,128)S(1)} %get-tuple-element.13.refs_1_, ...), custom_call_target="tpu_custom_call" | custom-call | tf_op jit(solution)/shard_map/pallas_call | solution.py:920

commit v5 on v4

--- a/solution.py
+++ b/solution.py
@@ -240,6 +240,62 @@
             src_ref=src, dst_ref=dst, send_sem=send, recv_sem=recv, device_id=device, device_id_type=MESH
         )
 
+    barrier = pltpu.get_barrier_semaphore()
+
+    def greet(**device):
+        pl.semaphore_signal(barrier, inc=1, device_id=device, device_id_type=MESH)
+
+    def bits(value, size):
+        return [lax.rem(value // 2**k, 2) for k in range(size.bit_length() - 1)]
+
+    def flip(value, digits, mask):
+        return value + sum((1 - 2 * digit) * 2**k for k, digit in enumerate(digits) if mask >> k & 1)
+
+    def reach(mask):
+        return (0, 1, 2, 3, 4, 3, 2, 3)[mask] if mask < 8 else 1 + reach(mask - 8)
+
+    def plane_reach(mask):
+        return sum((0, 1, 2, 1)[part] for part in (mask // ny, mask % ny))
+
+    x, y = ens * 2 + lon // nz, lat // 2
+    x_bits, y_bits, lon_bits = bits(x, 2 * nens), bits(y, ny), bits(lon, nlon)
+    plane_masks = sorted(range(1, plane), key=plane_reach, reverse=True)
+    column_masks = sorted(range(1, nz), key=reach, reverse=True)
+    lon_masks = sorted(range(1, nlon), key=reach, reverse=True)
+
+    def plane_peer(mask):
+        px, py = flip(x, x_bits, mask // ny), flip(y, y_bits, mask % ny)
+        device = dict(lon=lax.rem(px, 2) * nz + z, lat=py * 2 + core, ens=px // 2)
+        return px * ny + py, device
+
+    def lon_peer(mask):
+        return flip(lon, lon_bits, mask)
+
+
+    @pl.when(lat == top)
+    def _():
+        for mask in lon_masks:
+            greet(lon=lon_peer(mask))
+
+    for mask in plane_masks:
+        greet(**plane_peer(mask)[1])
+    for mask in column_masks:
+        greet(lon=lon_peer(mask))
+    greet(lon=left)
+    greet(lon=right)
+
+    @pl.when(lat > 0)
+    def _():
+        greet(lat=lat - 1)
+        greet(lon=left, lat=lat - 1)
+        greet(lon=right, lat=lat - 1)
+
+    @pl.when(lat < top)
+    def _():
+        greet(lat=lat + 1)
+        greet(lon=left, lat=lat + 1)
+        greet(lon=right, lat=lat + 1)
+
     loads = [
         (temp.at[0], trac.at[0, :, 8:24, :]),
         (height.at[0], surf.at[0, 0, 16:32, :]),
@@ -256,61 +312,6 @@
     loads = [pltpu.make_async_copy(src, dst, load_sem.at[k]) for k, (src, dst) in enumerate(loads)]
     for load in loads:
         load.start()
-
-    barrier = pltpu.get_barrier_semaphore()
-
-    def greet(**device):
-        pl.semaphore_signal(barrier, inc=1, device_id=device, device_id_type=MESH)
-
-    def bits(value, size):
-        return [lax.rem(value // 2**k, 2) for k in range(size.bit_length() - 1)]
-
-    def flip(value, digits, mask):
-        return value + sum((1 - 2 * digit) * 2**k for k, digit in enumerate(digits) if mask >> k & 1)
-
-    def reach(mask):
-        return (0, 1, 2, 3, 4, 3, 2, 3)[mask] if mask < 8 else 1 + reach(mask - 8)
-
-    def plane_reach(mask):
-        return sum((0, 1, 2, 1)[part] for part in (mask // ny, mask % ny))
-
-    x, y = ens * 2 + lon // nz, lat // 2
-    x_bits, y_bits, lon_bits = bits(x, 2 * nens), bits(y, ny), bits(lon, nlon)
-    plane_masks = sorted(range(1, plane), key=plane_reach, reverse=True)
-    column_masks = sorted(range(1, nz), key=reach, reverse=True)
-    lon_masks = sorted(range(1, nlon), key=reach, reverse=True)
-
-    def plane_peer(mask):
-        px, py = flip(x, x_bits, mask // ny), flip(y, y_bits, mask % ny)
-        device = dict(lon=lax.rem(px, 2) * nz + z, lat=py * 2 + core, ens=px // 2)
-        return px * ny + py, device
-
-    def lon_peer(mask):
-        return flip(lon, lon_bits, mask)
-
-    for mask in plane_masks:
-        greet(**plane_peer(mask)[1])
-    for mask in column_masks:
-        greet(lon=lon_peer(mask))
-    greet(lon=left)
-    greet(lon=right)
-
-    @pl.when(lat > 0)
-    def _():
-        greet(lat=lat - 1)
-        greet(lon=left, lat=lat - 1)
-        greet(lon=right, lat=lat - 1)
-
-    @pl.when(lat < top)
-    def _():
-        greet(lat=lat + 1)
-        greet(lon=left, lat=lat + 1)
-        greet(lon=right, lat=lat + 1)
-
-    @pl.when(lat == top)
-    def _():
-        for mask in lon_masks:
-            greet(lon=lon_peer(mask))
 
     inputs[:, 32 * (HCH + 1) :, :] = jnp.zeros((2, 32 * (15 - HCH), LANES), F32)
     for ref, rows in ((gs3, 20), (gs2, 22), (gs1, 24)):
@@ -764,10 +765,18 @@
 
     for_lat(sent_back)
 
+    @pl.when(lat == top)
+    def _():
+        for mask in lon_masks:
+            for part, ref in enumerate((unfold_surf, unfold_trac)):
+                lon_copy(ref, mask, unfold_send.at[part], unfold_recv.at[part]).wait_send()
+
     for mask in plane_masks:
         plane_copy(mask, True).wait_recv()
     totals[core] = sum_slots(plane_in, plane)
     total_copy().start()
+    for mask in plane_masks:
+        plane_copy(mask).wait_send()
 
     @pl.when(lat == top)
     def _():
@@ -808,15 +817,7 @@
         first_out[:, 11 * tap : 11 * tap + CL] = block[:, 0:CL]
         first_out[:, 11 * tap + CL : 11 * tap + CL + 1] = block[:, HCH : HCH + 1]
 
-    for mask in plane_masks:
-        plane_copy(mask).wait_send()
     total_copy().wait_send()
-
-    @pl.when(lat == top)
-    def _():
-        for mask in lon_masks:
-            for part, ref in enumerate((unfold_surf, unfold_trac)):
-                lon_copy(ref, mask, unfold_send.at[part], unfold_recv.at[part]).wait_send()
 
 
 def hand_over(*refs):

time: 39.1 us -> 38.8 us (level)
  no operation moved by 1% of the time
where the time goes in v5:
time: 38.8 us; the launch traced here: 38.7 us
  Pallas kernels  38 us (98%)
  between operations  0.64 us (2%)
    pallas_call x1, Pallas kernels, local(): pl.pallas_call(functools.partial(kernel, (nlon, nlat, nens)), out_shape=t...  37.3 us

profile of v5, /device:TPU:1, one launch (start us, length us, event | category | flops | bytes accessed | tf_op | source)
XLA Modules:
  0.0 38.7 jit_solution(14470409589954756698)
XLA Ops:
  0.6 37.3 %shard_map.154 = (f32[1,12,16,128]{3,2,1,0:T(8,128)S(1)}, f32[1,16,128]{2,1,0:T(8,128)S(1)}, f32[1,2,16,128]{3,2,1,0:T(8,128)S(1)}, f32[16,99]{1,0:T(8,128)S(1)}...) custom-call(f32[1,12,16,128]{3,2,1,0:T(8,128)} %temp.1, f32[1,16,128]{2,1,0:T(8,128)} %height.1, f32[1,2,16,128]{3,2,1,0:T(8,128)} %flow.1, ...), custom_call_target="tpu_custom_call" | custom-call | tf_op jit(solution)/shard_map/pallas_call | solution.py:911
  38.0 0.7 %shard_map.155 = (f32[1,12,16,128]{3,2,1,0:T(8,128)}, f32[1,16,128]{2,1,0:T(8,128)}, f32[1,2,16,128]{3,2,1,0:T(8,128)}, f32[16,99]{1,0:T(8,128)}, f32[16,144]{1,0:T(8,128)}, /*index=5*/f32[10,144]{1,0:T(8,128)}) custom-call(f32[1,12,16,128]{3,2,1,0:T(8,128)S(1)} %get-tuple-element.12.refs_0_, f32[1,16,128]{2,1,0:T(8,128)S(1)} %get-tuple-element.13.refs_1_, ...), custom_call_target="tpu_custom_call" | custom-call | tf_op jit(solution)/shard_map/pallas_call | solution.py:921

commit v6 on v5

--- a/solution.py
+++ b/solution.py
@@ -590,6 +590,11 @@
 
     half_copy().start()
 
+    half_copy().wait_recv()
+    column_in[z] = halves[core] + half_in[...]
+    for mask in column_masks:
+        column_copy(mask).start()
+
     for row in range(22):
         grad = conv_row(flip1, gs1, row)
         for tile in range(2):
@@ -641,11 +646,6 @@
             out[lon, row : row + 1, :] = grads[0, f, first + m : first + m + 1, :]
             edge[row : row + 1, :] = grads[1, f, first + m : first + m + 1, :]
         out[lon, 32:40, :] = pack_edges([edge[8 * g : 8 * g + 8, :] for g in range(4)], width)
-
-    half_copy().wait_recv()
-    column_in[z] = halves[core] + half_in[...]
-    for mask in column_masks:
-        column_copy(mask).start()
 
     @pl.when(lat == top)
     def _():

time: 38.8 us -> 38.7 us (level)
  no operation moved by 1% of the time
where the time goes in v6:
time: 38.7 us; the launch traced here: 38.6 us
  Pallas kernels  38 us (98%)
  between operations  0.64 us (2%)
    pallas_call x1, Pallas kernels, local(): pl.pallas_call(functools.partial(kernel, (nlon, nlat, nens)), out_shape=t...  37.3 us

profile of v6, /device:TPU:1, one launch (start us, length us, event | category | flops | bytes accessed | tf_op | source)
XLA Modules:
  0.0 38.6 jit_solution(9172262690273336986)
XLA Ops:
  0.6 37.3 %shard_map.154 = (f32[1,12,16,128]{3,2,1,0:T(8,128)S(1)}, f32[1,16,128]{2,1,0:T(8,128)S(1)}, f32[1,2,16,128]{3,2,1,0:T(8,128)S(1)}, f32[16,99]{1,0:T(8,128)S(1)}...) custom-call(f32[1,12,16,128]{3,2,1,0:T(8,128)} %temp.1, f32[1,16,128]{2,1,0:T(8,128)} %height.1, f32[1,2,16,128]{3,2,1,0:T(8,128)} %flow.1, ...), custom_call_target="tpu_custom_call" | custom-call | tf_op jit(solution)/shard_map/pallas_call | solution.py:911
  37.9 0.7 %shard_map.155 = (f32[1,12,16,128]{3,2,1,0:T(8,128)}, f32[1,16,128]{2,1,0:T(8,128)}, f32[1,2,16,128]{3,2,1,0:T(8,128)}, f32[16,99]{1,0:T(8,128)}, f32[16,144]{1,0:T(8,128)}, /*index=5*/f32[10,144]{1,0:T(8,128)}) custom-call(f32[1,12,16,128]{3,2,1,0:T(8,128)S(1)} %get-tuple-element.12.refs_0_, f32[1,16,128]{2,1,0:T(8,128)S(1)} %get-tuple-element.13.refs_1_, ...), custom_call_target="tpu_custom_call" | custom-call | tf_op jit(solution)/shard_map/pallas_call | solution.py:921
